TPU v7x, 512 devices: a whole 4x8x8 slice. The times are simulated.
512 devices in a mesh: segment: 2 (over x_lo), dc: 32 (over x_hi, z, core), head: 8 (over y).
Axes of the slice: x: 4 (x_hi: 2, x_lo: 2; x = x_hi * 2 + x_lo), y: 8, z: 8, core: 2. Of those that a mesh axis runs over, the one named last changes fastest.
Arguments:
- queries: bfloat16 [2, 2, 2048, 8192], P('segment', None, 'dc', 'head'), may hold values from -160 to 160
- keys: bfloat16 [2, 2, 2048, 1024], P('segment', None, 'dc', 'head'), may hold values from -6 to 6
- values: bfloat16 [2, 2, 2048, 1024], P('segment', None, 'dc', 'head'), may hold values from -18 to 18
- block_order: int32 [2, 64], replicated, may hold values from 0 to 63, each once within a row
- doc_lengths: int32 [2, 16], replicated, may hold values from 1 to 1024, 2048 in all within a row
Outputs:
- attended: bfloat16 [2, 2, 2048, 8192], P('segment', None, 'dc', 'head')
Inputs may be any that keep to these rules, and one draw needn't show every extreme that they name: `block_order`: slots g of dc index r run over blocks 2r and 2r + 1 of the row: the row is a permutation of the blocks of 32 pack positions. `doc_lengths`: each row sums to 2048; its largest entry is exactly 1024.
All inputs are finite; a program needn't handle non-finite values.
Results may differ from a plain program's by a relative error of at most 0.013.
Values may be sent and summed in bfloat16 or wider, within the bound.
A program may use at most 64 MiB of HBM per device.

v0:
```python
import math

import jax
import jax.numpy as jnp
from jax import lax
from jax.sharding import PartitionSpec as P

HEAD_DIM = 128


NEG_FILL = -1e30


def shifted(value, axis, steps):
    count = lax.axis_size(axis)
    first, last = (max(0, -steps), min(count, count - steps))
    return lax.ppermute(value, axis, [(source, source + steps) for source in range(first, last)])


def locate(order_row, ends_row, start, count, block_size):
    slots = start + jnp.arange(count, dtype=jnp.int32)
    which_block = slots // block_size
    numbers = jnp.arange(order_row.shape[0], dtype=jnp.int32)
    picked = jnp.sum(
        jnp.where(which_block[:, None] == numbers[None, :], order_row[None, :], 0), axis=1
    )
    position = picked * block_size + slots % block_size
    document = jnp.sum((position[:, None] >= ends_row[None, :]).astype(jnp.int32), axis=1)
    return (position, document)


def attend_rows(query_rows, query_pos, query_doc, order_row, ends_row, block_size, key_source):
    rows, query_width = query_rows.shape
    kv_width = key_source[1]
    kv_local = kv_width // HEAD_DIM
    group_size = query_width // kv_width
    scale_factor = 1.0 / math.sqrt(HEAD_DIM)
    grouped_query = query_rows.reshape(rows, kv_local, group_size, HEAD_DIM)

    def compute(carry, key_piece, value_piece, visible):
        running_max, running_total, running_acc = carry
        scores = (
            jnp.einsum(
                "thgd,shd->hgts", grouped_query, key_piece, preferred_element_type=jnp.float32
            )
            * scale_factor
        )
        scores = jnp.where(visible[None, None], scores, NEG_FILL)
        new_max = jnp.maximum(running_max, jnp.max(scores, axis=3))
        weights = jnp.where(visible[None, None], jnp.exp(scores - new_max[..., None]), 0.0)
        new_total = jnp.sum(weights, axis=3)
        update = jnp.einsum(
            "hgts,shd->thgd",
            weights.astype(jnp.bfloat16),
            value_piece,
            preferred_element_type=jnp.float32,
        )
        return (new_max, new_total, update)

    def fold_step(carry, piece, start):
        key_block, value_block = piece
        count = key_block.shape[0]
        key_piece = key_block.reshape(count, kv_local, HEAD_DIM)
        value_piece = value_block.reshape(count, kv_local, HEAD_DIM)
        key_pos, key_doc = locate(order_row, ends_row, start, count, block_size)
        visible = (query_doc[:, None] == key_doc[None, :]) & (
            key_pos[None, :] <= query_pos[:, None]
        )
        return compute(carry, key_piece, value_piece, visible)

    initial = (
        jnp.full((kv_local, group_size, rows), NEG_FILL, jnp.float32),
        jnp.zeros((kv_local, group_size, rows), jnp.float32),
        jnp.zeros((rows, kv_local, group_size, HEAD_DIM), jnp.float32),
    )
    final_max, final_total, final_acc = key_source[0](fold_step, initial)
    mixed = final_acc / jnp.transpose(final_total, (2, 0, 1))[..., None]
    return mixed.reshape(rows, query_width).astype(jnp.bfloat16)


def cycle_source(key_rows, value_rows):

    def source_fold(fold_step, initial):
        return fold_step(
            initial,
            (
                lax.all_gather(key_rows, "dc", axis=0, tiled=True),
                lax.all_gather(value_rows, "dc", axis=0, tiled=True),
            ),
            jnp.int32(0),
        )

    return source_fold


def lift_rows(query_rows, incoming, total_features):
    widened = incoming.astype(jnp.float32)
    squares = lax.psum(jnp.sum(widened * widened, axis=1), "head")
    norm_scale = lax.rsqrt(squares / total_features + 1e-05)
    return (query_rows.astype(jnp.float32) + widened * norm_scale[:, None]).astype(jnp.bfloat16)


def on_device(queries, keys, values, block_order, doc_lengths):
    micro_count = queries.shape[1]
    rows = queries.shape[2]
    query_width = queries.shape[3]
    kv_width = keys.shape[3]
    block_size = rows // 2
    dc_rank = lax.axis_index("dc")
    segment_rank = lax.axis_index("segment")
    total_features = query_width * lax.axis_size("head")
    results = jnp.zeros((micro_count, rows, query_width), jnp.bfloat16)
    incoming = jnp.zeros((rows, query_width), jnp.bfloat16)
    for moment in range(micro_count + 1):
        micro = moment - segment_rank
        is_valid = (micro >= 0) & (micro < micro_count)
        picked = jnp.clip(micro, 0, micro_count - 1)
        query_rows = lax.dynamic_index_in_dim(queries[0], picked, 0, keepdims=False)
        key_rows = lax.dynamic_index_in_dim(keys[0], picked, 0, keepdims=False)
        value_rows = lax.dynamic_index_in_dim(values[0], picked, 0, keepdims=False)
        order_row = lax.dynamic_index_in_dim(block_order, picked, 0, keepdims=False)
        ends_row = jnp.cumsum(lax.dynamic_index_in_dim(doc_lengths, picked, 0, keepdims=False))
        query_pos, query_doc = locate(order_row, ends_row, dc_rank * rows, rows, block_size)
        lifted = lift_rows(query_rows, incoming, total_features)
        source_fold = cycle_source(key_rows, value_rows)
        output_rows = attend_rows(
            lifted, query_pos, query_doc, order_row, ends_row, block_size, (source_fold, kv_width)
        )
        results = jnp.where(
            is_valid, lax.dynamic_update_index_in_dim(results, output_rows, picked, 0), results
        )
        if moment < micro_count:
            incoming = shifted(output_rows, "segment", 1)
    return results[None]


def solution(mesh):
    placed = (
        P("segment", None, "dc", "head"),
        P("segment", None, "dc", "head"),
        P("segment", None, "dc", "head"),
        P(),
        P(),
    )
    return jax.shard_map(
        on_device,
        mesh=mesh,
        in_specs=placed,
        out_specs=P("segment", None, "dc", "head"),
        check_vma=False,
    )
```

profile of v0, /device:TPU:66, one launch (start us, length us, event | category | flops | bytes accessed | tf_op | source)
XLA Modules:
  0.0 302.2 jit_solution(17043633983610018919)
XLA Ops:
  0.0 0.8 fusion.80
  0.8 0.2 select_reduce_fusion.3
  1.0 0.8 fusion.85
  1.9 0.1 copy.22
  2.0 0.1 reduce.6
  2.1 0.3 select_reduce_fusion
  2.4 0.1 convert_reduce_fusion.5
  2.5 0.1 convert_reduce_fusion.2
  2.6 0.8 constant_dynamic-slice_fusion
  3.4 0.0 copy-start.1
  3.4 43.1 %all-gather.1 = bf16[1,1,2048,128]{3,2,1,0:T(8,128)(2,1)S(1)} all-gather(bf16[1,1,64,128]{3,2,1,0:T(8,128)(2,1)S(1)} %get-tuple-element.15), channel_id=3, replica_groups=mesh['segment'=2,'dc'=32,'head'=8] {'dc'}, dimensions={2}, use_global_device_ids=true | all-gather | bytes 540672 | tf_op jit(solution)/shard_map/all_gather | solution.py:87
  46.5 0.9 dynamic-slice_bitcast_fusion
  47.4 0.2 compare_and_fusion.2
  47.6 0.9 fusion
  48.5 0.0 copy-start
  48.5 0.0 copy-done.1
  48.6 42.9 %all-gather = bf16[1,1,2048,128]{3,2,1,0:T(8,128)(2,1)S(1)} all-gather(bf16[1,1,64,128]{3,2,1,0:T(8,128)(2,1)S(1)} %get-tuple-element.12), channel_id=2, replica_groups=mesh['segment'=2,'dc'=32,'head'=8] {'dc'}, dimensions={2}, use_global_device_ids=true | all-gather | bytes 540672 | tf_op jit(solution)/shard_map/all_gather | solution.py:88
  91.5 0.0 copy-done
  91.5 1.3 fusion.3
  92.7 3.2 %broadcast_select_fusion = (bf16[64,1,8,128]{3,0,2,1:T(8,128)(2,1)S(1)}, bf16[64,1,8,128]{3,0,2,1:T(8,128)(2,1)S(1)}) fusion(pred[]{:T(512)S(6)} %and.136, f32[64,8]{0,1:T(8,128)S(1)} %bitcast.249, f32[2048,64,8]{0,1,2:T(8,128)} %copy-done, f32[8,64]{1,0:T(8,128)S(1)} %broadcast_maximum_fusion.2, pred[64,2048]{1,0:T(8,128)(4,1)S(1)} %compare_and_fusion.2, ...), kind=kOutput, calls=%fused_computation.74 | convolution fusion | flops 273874944 | bytes 5115905 | tf_op jit(solution)/shard_map/hgts,shd->thgd/dot_general | solution.py:52
  96.0 0.0 copy-start.2
  96.0 0.1 copy.26
  96.1 1.3 collective-permute-start
  97.4 0.1 copy.25
  97.5 0.1 reduce.7
  97.7 0.1 convert_reduce_fusion.4
  97.7 0.1 convert_reduce_fusion.1
  97.8 38.1 %all-gather.3 = bf16[1,1,2048,128]{3,2,1,0:T(8,128)(2,1)S(1)} all-gather(bf16[1,1,64,128]{3,2,1,0:T(8,128)(2,1)S(1)} %get-tuple-element.16), channel_id=5, replica_groups=mesh['segment'=2,'dc'=32,'head'=8] {'dc'}, dimensions={2}, use_global_device_ids=true | all-gather | bytes 540672 | tf_op jit(solution)/shard_map/all_gather | solution.py:87
  136.0 39.4 %all-gather.2 = bf16[1,1,2048,128]{3,2,1,0:T(8,128)(2,1)S(1)} all-gather(bf16[1,1,64,128]{3,2,1,0:T(8,128)(2,1)S(1)} %get-tuple-element.13), channel_id=4, replica_groups=mesh['segment'=2,'dc'=32,'head'=8] {'dc'}, dimensions={2}, use_global_device_ids=true | all-gather | bytes 540672 | tf_op jit(solution)/shard_map/all_gather | solution.py:88
  175.4 0.1 copy.29
  175.6 0.1 reduce.8
  175.7 0.1 convert_reduce_fusion.3
  175.8 0.1 convert_reduce_fusion
  175.9 38.1 %all-gather.5 = bf16[1,1,2048,128]{3,2,1,0:T(8,128)(2,1)S(1)} all-gather(bf16[1,1,64,128]{3,2,1,0:T(8,128)(2,1)S(1)} %get-tuple-element.14), channel_id=7, replica_groups=mesh['segment'=2,'dc'=32,'head'=8] {'dc'}, dimensions={2}, use_global_device_ids=true | all-gather | bytes 540672 | tf_op jit(solution)/shard_map/all_gather | solution.py:87
  214.0 0.2 compare_and_fusion.1
  214.2 0.2 compare_and_fusion
  214.4 39.5 %all-gather.4 = bf16[1,1,2048,128]{3,2,1,0:T(8,128)(2,1)S(1)} all-gather(bf16[1,1,64,128]{3,2,1,0:T(8,128)(2,1)S(1)} %get-tuple-element.11), channel_id=6, replica_groups=mesh['segment'=2,'dc'=32,'head'=8] {'dc'}, dimensions={2}, use_global_device_ids=true | all-gather | bytes 540672 | tf_op jit(solution)/shard_map/all_gather | solution.py:88
  253.8 0.1 copy.24
  253.9 0.1 select_n.188
  254.1 0.0 collective-permute-done
  254.1 0.1 fusion.57
  254.2 17.6 %psum.14 = f32[64]{0:T(128)S(1)} all-reduce(f32[64]{0:T(128)S(1)} %fusion.57), channel_id=1, replica_groups=mesh['segment'=2,'dc'=32,'head'=8] {'head'}, use_global_device_ids=true, to_apply=%region_13.14 | all-reduce | flops 64 | bytes 512 | tf_op jit(solution)/shard_map/psum | solution.py:98
  271.8 0.0 copy-done.2
  271.8 1.0 fusion.1
  272.8 1.3 fusion.5
  274.1 1.1 fusion.39
  275.1 0.1 copy.28
  275.2 0.1 convert_element_type.118
  275.3 1.3 collective-permute-start.1
  276.7 0.7 copy.60
  277.4 5.4 %collective-permute-done.1 = bf16[64,1024]{1,0:T(8,128)(2,1)S(1)} collective-permute-done((bf16[64,1024]{1,0:T(8,128)(2,1)S(1)}, bf16[64,1024]{1,0:T(8,128)(2,1)S(1)}, u32[]{:S(2)}, u32[]{:S(2)}) %collective-permute-start.1) | collective-permute-done | bytes 131104 | tf_op jit(solution)/shard_map/ppermute | solution.py:17
  282.8 0.1 fusion.60
  282.9 15.1 %psum.18 = f32[64]{0:T(128)S(1)} all-reduce(f32[64]{0:T(128)S(1)} %fusion.60), channel_id=1, replica_groups=mesh['segment'=2,'dc'=32,'head'=8] {'head'}, use_global_device_ids=true, to_apply=%region_22.23 | all-reduce | flops 64 | bytes 512 | tf_op jit(solution)/shard_map/psum | solution.py:98
  298.1 1.0 fusion.2
  299.0 1.3 fusion.7
  300.3 1.1 fusion.45
  301.4 0.1 copy.32
  301.5 0.1 convert_element_type.128
  301.5 0.7 bitcast_dynamic-update-slice_fusion
  (23 shorter events, 0.4 us)
Async XLA Ops:
  3.4 45.1 %copy-start.1 = (bf16[1,2,64,128]{3,2,1,0:T(8,128)(2,1)S(1)}, bf16[1,2,64,128]{3,2,1,0:T(8,128)(2,1)}, u32[]{:S(2)}) copy-start(bf16[1,2,64,128]{3,2,1,0:T(8,128)(2,1)} %param.7) | copy-start | bytes 98308
  48.5 42.9 %copy-start = (f32[2048,64,8]{0,1,2:T(8,128)}, f32[2048,64,8]{0,1,2:T(8,128)S(1)}, u32[]{:S(2)}) copy-start(f32[2048,64,8]{0,1,2:T(8,128)S(1)} %get-tuple-element.24) | copy-start | bytes 12582916
  96.0 175.9 %copy-start.2 = (bf16[1,2,64,1024]{3,2,1,0:T(8,128)(2,1)S(1)}, bf16[1,2,64,1024]{3,2,1,0:T(8,128)(2,1)}, u32[]{:S(2)}) copy-start(bf16[1,2,64,1024]{3,2,1,0:T(8,128)(2,1)} %param.5) | copy-start | bytes 786436
  96.1 158.0 %collective-permute-start = (bf16[64,1024]{1,0:T(8,128)(2,1)S(1)}, bf16[64,1024]{1,0:T(8,128)(2,1)S(1)}, u32[]{:S(2)}, u32[]{:S(2)}) collective-permute-start(bf16[64,1024]{1,0:T(8,128)(2,1)S(1)} %bitcast.247), channel_id=1, source_target_pairs={{0,256},{1,257},{2,258},{3,259},{4,260},{5,261},{6,262},{7,263},{8... | collective-permute-start | bytes 393224 | tf_op jit(solution)/shard_map/ppermute | solution.py:17
  275.3 7.5 %collective-permute-start.1 = (bf16[64,1024]{1,0:T(8,128)(2,1)S(1)}, bf16[64,1024]{1,0:T(8,128)(2,1)S(1)}, u32[]{:S(2)}, u32[]{:S(2)}) collective-permute-start(bf16[64,1024]{1,0:T(8,128)(2,1)S(1)} %bitcast.248), channel_id=1, source_target_pairs={{0,256},{1,257},{2,258},{3,259},{4,260},{5,261},{6,262},{7,263},{8... | collective-permute-start | bytes 393224 | tf_op jit(solution)/shard_map/ppermute | solution.py:17
where the time goes:
time: 303 us; the launch traced here: 302 us
  blocking collectives  274 us (90%)
  matrix products  8.18 us (3%)
  other arithmetic  6.96 us (2%)
  waiting for transfers between devices  5.42 us (2%)
  local copies, waits for them, and re-layouts  4.96 us (2%)
    all_gather x3, blocking collectives, source_fold(): lax.all_gather(value_rows, 'dc', axis=0, tiled=True)  122 us
    all_gather x3, blocking collectives, source_fold(): lax.all_gather(key_rows, 'dc', axis=0, tiled=True)  119 us
    psum x2, blocking collectives, lift_rows(): squares = lax.psum(jnp.sum(widened * widened, axis=1), 'head')  32.7 us
  transfers between devices with their start and end apart: 2, of which 1 were waited for; matrix products, arithmetic and copies ran while one was open for 1% of the time, Pallas kernels for 0%

commit v1 on v0

v1 whole, which is shorter than its diff:
```python
import math

import jax
import jax.numpy as jnp
from jax import lax
from jax.experimental import pallas as pl
from jax.experimental.pallas import tpu as pltpu
from jax.sharding import PartitionSpec as P

HEAD_DIM = 128
BLOCK = 32
MICRO = 2
DOCS = 16
HEADS_LOCAL = 8
N_HEAD = 8
ROWS = 64
FEATURES = 8192
NZ = 8
FAR = NZ // 2
PLUS, MINUS = 0, 1
HIDDEN = -1e30
MESH = pl.DeviceIdType.MESH
EXP_SCALE = math.log2(math.e) / math.sqrt(HEAD_DIM)
GROUP_ROWS = 256


def kernel(
    order_ref,
    lengths_ref,
    q_hbm,
    k_hbm,
    v_hbm,
    o_ref,
    q_ref,
    buf,
    key_mask,
    query_mask,
    qx,
    acc,
    peak,
    att,
    ss_out,
    ss_in,
    load_sem,
    z_send,
    z_recv,
    s_send,
    s_recv,
    x_send,
    x_recv,
    a_send,
    a_recv,
    n_send,
    n_recv,
):
    seg = lax.axis_index("segment")
    dc = lax.axis_index("dc")
    head = lax.axis_index("head")
    core = dc % 2
    z = (dc // 2) % NZ
    xh = dc // (2 * NZ)

    def place(x_hi, z_at, core_at):
        return (x_hi * NZ + z_at) * 2 + core_at

    def z_of(direction, distance):
        if direction == PLUS:
            return (z + NZ - distance) % NZ
        return (z + distance) % NZ

    sibling = (seg, place(xh, z, 1 - core), head)
    x_peer = (seg, place(1 - xh, z, core), head)
    z_next = (
        (seg, place(xh, (z + 1) % NZ, core), head),
        (seg, place(xh, (z + NZ - 1) % NZ, core), head),
    )

    loads = []
    for m in range(MICRO):
        mine = buf.at[m, core, z, xh]
        loads.append(
            (
                pltpu.make_async_copy(k_hbm.at[0, m], mine.at[0], load_sem.at[m, 0]),
                pltpu.make_async_copy(v_hbm.at[0, m], mine.at[1], load_sem.at[m, 1]),
                pltpu.make_async_copy(q_hbm.at[0, m], q_ref.at[m], load_sem.at[m, 2]),
            )
        )
    for one in range(3):
        for m in range(MICRO):
            loads[m][one].start()

    barrier = pltpu.get_barrier_semaphore()
    for device in (sibling, x_peer) + z_next:
        pl.semaphore_signal(barrier, inc=1, device_id=device, device_id_type=MESH)
    for h in range(N_HEAD):
        pl.semaphore_signal(
            barrier, inc=1, device_id=(1 - seg, dc, h), device_id_type=MESH
        )
    pl.semaphore_wait(barrier, 4 + N_HEAD)

    def shard_x(part):
        return xh if part == 0 else 1 - xh

    def z_copy(m, direction, distance, part):
        source_z = z_of(direction, distance - 1)
        block = buf.at[m, core, source_z, shard_x(part)]
        return pltpu.make_async_remote_copy(
            src_ref=block,
            dst_ref=block,
            send_sem=z_send.at[m, direction, distance - 1, part],
            recv_sem=z_recv.at[m, direction, distance - 1, part],
            device_id=z_next[direction],
            device_id_type=MESH,
        )

    def s_copy(m, direction, distance, part):
        block = buf.at[m, core, z_of(direction, distance), shard_x(part)]
        return pltpu.make_async_remote_copy(
            src_ref=block,
            dst_ref=block,
            send_sem=s_send.at[m, direction, distance, part],
            recv_sem=s_recv.at[m, direction, distance, part],
            device_id=sibling,
            device_id_type=MESH,
        )

    def x_copy(m):
        block = buf.at[m, core, z, xh]
        return pltpu.make_async_remote_copy(
            src_ref=block,
            dst_ref=block,
            send_sem=x_send.at[m],
            recv_sem=x_recv.at[m],
            device_id=x_peer,
            device_id_type=MESH,
        )

    def travels(direction, distance, part):
        return distance < FAR or direction == part

    def offer_own(m):
        loads[m][0].wait()
        loads[m][1].wait()
        x_copy(m).start()
        z_copy(m, PLUS, 1, 0).start()
        z_copy(m, MINUS, 1, 0).start()
        s_copy(m, PLUS, 0, 0).start()

    def pass_x(m):
        x_copy(m).wait_recv()
        z_copy(m, PLUS, 1, 1).start()
        z_copy(m, MINUS, 1, 1).start()
        s_copy(m, PLUS, 0, 1).start()

    def pass_z(m, distance, part):
        for direction in (PLUS, MINUS):
            if travels(direction, distance, part):
                z_copy(m, direction, distance, part).wait_recv()
                if distance < FAR and travels(direction, distance + 1, part):
                    z_copy(m, direction, distance + 1, part).start()
                s_copy(m, direction, distance, part).start()

    def wait_sibling(m, distance):
        for part in (0, 1):
            for direction in (PLUS, MINUS):
                if distance == 0:
                    if direction == PLUS:
                        s_copy(m, PLUS, 0, part).wait_recv()
                elif travels(direction, distance, part):
                    s_copy(m, direction, distance, part).wait_recv()

    def finish_sends(m):
        x_copy(m).wait_send()
        for part in (0, 1):
            s_copy(m, PLUS, 0, part).wait_send()
            for distance in range(1, FAR + 1):
                for direction in (PLUS, MINUS):
                    if travels(direction, distance, part):
                        z_copy(m, direction, distance, part).wait_send()
                        s_copy(m, direction, distance, part).wait_send()

    def build_masks(m):
        lane = lax.broadcasted_iota(jnp.int32, (1, 128), 1)
        none = jnp.int32(1 << 20)
        low = jnp.full((1, 128), none, jnp.int32)
        high = jnp.zeros((1, 128), jnp.int32)
        run = jnp.int32(0)
        for d in range(DOCS):
            low = jnp.where(lane == d, run, low)
            run = run + lengths_ref[m, d]
            high = jnp.where(lane == d, run, high)
        for half in range(2):
            first = order_ref[m, dc * 2 + half] * BLOCK
            low = jnp.where(lane == DOCS + half, first + BLOCK, low)
            high = jnp.where(lane == DOCS + half, none, high)
            fine = (lane >= 32 + 32 * half) & (lane < 64 + 32 * half)
            low = jnp.where(fine, first + lane - (32 + 32 * half), low)
            high = jnp.where(fine, first + lane - (31 + 32 * half), high)
        high_q = jnp.where(lane < DOCS, high, none)
        row = lax.broadcasted_iota(jnp.int32, (BLOCK, 128), 0)
        for half in range(2):
            pos = order_ref[m, dc * 2 + half] * BLOCK + row
            hidden = (pos < low) | (pos >= high_q)
            query_mask[m, half * BLOCK : (half + 1) * BLOCK, :] = jnp.where(
                hidden, HIDDEN, 0.0
            ).astype(jnp.bfloat16)

        def one_z(z_at, carry):
            for c_at in range(2):
                for x_at in range(2):
                    for half in range(2):
                        number = place(x_at, z_at, c_at) * 2 + half
                        pos = order_ref[m, number] * BLOCK + row
                        inside = (pos >= low) & (pos < high)
                        key_mask[
                            m, z_at, c_at, x_at, half * BLOCK : (half + 1) * BLOCK, :
                        ] = jnp.where(inside, 1.0, 0.0).astype(jnp.bfloat16)
            return carry

        lax.fori_loop(0, NZ, one_z, 0)

    def start_rows(first, count):
        acc[first : first + count, :] = jnp.zeros((count, 256), jnp.float32)
        peak[first : first + count, :] = jnp.full((count, 128), HIDDEN, jnp.float32)

    def fold(m, z_list, first, count):
        keys, values = [], []
        for z_at in z_list:
            k = buf[m, :, z_at, :, 0].reshape(256, HEAD_DIM)
            v = buf[m, :, z_at, :, 1].reshape(256, HEAD_DIM)
            b = key_mask[m, z_at].reshape(256, 128)
            keys.append(jnp.concatenate([k, b], axis=1))
            values.append(jnp.concatenate([v, jnp.ones_like(v)], axis=1))
        kx = jnp.concatenate(keys, axis=0) if len(keys) > 1 else keys[0]
        vx = jnp.concatenate(values, axis=0) if len(values) > 1 else values[0]
        for start in range(first, first + count, GROUP_ROWS):
            rows = slice(start, start + GROUP_ROWS)
            scores = lax.dot_general(
                qx[rows, :], kx, (((1,), (1,)), ((), ())), preferred_element_type=jnp.float32
            )
            old = peak[rows, :]
            new = jnp.maximum(old, jnp.max(scores, axis=1, keepdims=True))
            peak[rows, :] = new
            weights = jnp.exp2((scores - new[:, :1]) * EXP_SCALE).astype(jnp.bfloat16)
            fade = jnp.exp2((old - new) * EXP_SCALE)
            acc[rows, :] = acc[rows, :] * jnp.concatenate([fade, fade], axis=1) + jnp.dot(
                weights, vx, preferred_element_type=jnp.float32
            )

    def finished(m, h):
        rows = slice(h * ROWS, (h + 1) * ROWS)
        out = (acc[rows, :HEAD_DIM] / acc[rows, HEAD_DIM:]).astype(jnp.bfloat16)
        o_ref[0, m, :, h * HEAD_DIM : (h + 1) * HEAD_DIM] = out
        return out

    def a_copy(m, h):
        return pltpu.make_async_remote_copy(
            src_ref=att.at[m, h],
            dst_ref=att.at[m, h],
            send_sem=a_send.at[m, h],
            recv_sem=a_recv.at[m, h],
            device_id=(1, dc, head),
            device_id_type=MESH,
        )

    def n_copy(m, h):
        return pltpu.make_async_remote_copy(
            src_ref=ss_out.at[m],
            dst_ref=ss_in.at[m, head],
            send_sem=n_send.at[m, h],
            recv_sem=n_recv.at[m, head],
            device_id=(1, dc, h),
            device_id_type=MESH,
        )

    def n_arrival(m, h):
        return pltpu.make_async_remote_copy(
            src_ref=ss_out.at[m],
            dst_ref=ss_in.at[m, h],
            send_sem=n_send.at[m, h],
            recv_sem=n_recv.at[m, h],
            device_id=(0, dc, h),
            device_id_type=MESH,
        )

    def stage_query(m, h, value):
        rows = slice(h * ROWS, (h + 1) * ROWS)
        qx[rows, :HEAD_DIM] = value
        qx[rows, HEAD_DIM:] = query_mask[m]

    def hand_over(m):
        squares = jnp.zeros((ROWS, HEAD_DIM), jnp.float32)
        for h in range(HEADS_LOCAL):
            out = finished(m, h)
            att[m, h] = out
            a_copy(m, h).start()
            wide = out.astype(jnp.float32)
            squares = squares + wide * wide
        ss_out[m, :, :ROWS] = jnp.sum(jnp.transpose(squares), axis=0, keepdims=True)
        for h in range(N_HEAD):
            n_copy(m, h).start()

    def near(distance):
        if distance == 0:
            return (z,)
        if distance == FAR:
            return (z_of(PLUS, FAR),)
        return (z_of(PLUS, distance), z_of(MINUS, distance))

    def compute(m, distance):
        wait_sibling(m, distance)
        fold(m, near(distance), 0, HEADS_LOCAL * ROWS)

    def begin(m):
        loads[m][2].wait()
        for h in range(HEADS_LOCAL):
            stage_query(m, h, q_ref[m, :, h * HEAD_DIM : (h + 1) * HEAD_DIM])
        start_rows(0, HEADS_LOCAL * ROWS)

    @pl.when(seg == 0)
    def _():
        offer_own(0)
        build_masks(0)
        begin(0)
        pass_x(0)
        pass_z(0, 1, 0)
        pass_z(0, 1, 1)
        compute(0, 0)
        pass_z(0, 2, 0)
        pass_z(0, 2, 1)
        offer_own(1)
        compute(0, 1)
        pass_z(0, 3, 0)
        pass_z(0, 3, 1)
        pass_x(1)
        compute(0, 2)
        pass_z(0, 4, 0)
        pass_z(0, 4, 1)
        pass_z(1, 1, 0)
        pass_z(1, 1, 1)
        compute(0, 3)
        compute(0, 4)
        hand_over(0)
        pass_z(1, 2, 0)
        pass_z(1, 2, 1)
        build_masks(1)
        begin(1)
        compute(1, 0)
        compute(1, 1)
        pass_z(1, 3, 0)
        pass_z(1, 3, 1)
        compute(1, 2)
        pass_z(1, 4, 0)
        pass_z(1, 4, 1)
        compute(1, 3)
        compute(1, 4)
        hand_over(1)
        for m in range(MICRO):
            finish_sends(m)
            for h in range(HEADS_LOCAL):
                a_copy(m, h).wait_send()
                n_copy(m, h).wait_send()

    @pl.when(seg == 1)
    def _():
        offer_own(0)
        build_masks(0)
        pass_x(0)
        for distance in range(1, FAR + 1):
            if distance == 3:
                offer_own(1)
            if distance == 4:
                pass_x(1)
            pass_z(0, distance, 0)
            pass_z(0, distance, 1)
        build_masks(1)
        for distance in range(1, FAR + 1):
            pass_z(1, distance, 0)
            pass_z(1, distance, 1)
        for m in range(MICRO):
            for distance in range(FAR + 1):
                wait_sibling(m, distance)
            finish_sends(m)
        for m in range(MICRO):
            loads[m][2].wait()
            for h in range(N_HEAD):
                n_arrival(m, h).wait_recv()
            total = ss_in[m, 0]
            for h in range(1, N_HEAD):
                total = total + ss_in[m, h]
            wide_total = jnp.broadcast_to(total[:, :ROWS], (HEAD_DIM, ROWS))
            norm = lax.rsqrt(jnp.transpose(wide_total) / FEATURES + 1e-05)
            start_rows(0, HEADS_LOCAL * ROWS)
            per_group = GROUP_ROWS // ROWS
            for group in range(HEADS_LOCAL // per_group):
                for h in range(group * per_group, (group + 1) * per_group):
                    a_copy(m, h).wait_recv()
                    lifted = (
                        q_ref[m, :, h * HEAD_DIM : (h + 1) * HEAD_DIM].astype(jnp.float32)
                        + att[m, h].astype(jnp.float32) * norm
                    )
                    stage_query(m, h, lifted.astype(jnp.bfloat16))
                for distance in range(FAR + 1):
                    fold(m, near(distance), group * GROUP_ROWS, GROUP_ROWS)
                for h in range(group * per_group, (group + 1) * per_group):
                    finished(m, h)


def on_device(queries, keys, values, block_order, doc_lengths):
    dma = pltpu.SemaphoreType.DMA
    z_shape = (MICRO, 2, FAR, 2)
    s_shape = (MICRO, 2, FAR + 1, 2)
    return pl.pallas_call(
        kernel,
        out_shape=jax.ShapeDtypeStruct(queries.shape, jnp.bfloat16),
        in_specs=[
            pl.BlockSpec(memory_space=pltpu.SMEM),
            pl.BlockSpec(memory_space=pltpu.SMEM),
            pl.BlockSpec(memory_space=pl.ANY),
            pl.BlockSpec(memory_space=pl.ANY),
            pl.BlockSpec(memory_space=pl.ANY),
        ],
        out_specs=pl.BlockSpec(memory_space=pltpu.VMEM),
        scratch_shapes=[
            pltpu.VMEM((MICRO, ROWS, HEADS_LOCAL * HEAD_DIM), jnp.bfloat16),
            pltpu.VMEM((MICRO, 2, NZ, 2, 2, ROWS, HEAD_DIM), jnp.bfloat16),
            pltpu.VMEM((MICRO, NZ, 2, 2, ROWS, 128), jnp.bfloat16),
            pltpu.VMEM((MICRO, ROWS, 128), jnp.bfloat16),
            pltpu.VMEM((HEADS_LOCAL * ROWS, 256), jnp.bfloat16),
            pltpu.VMEM((HEADS_LOCAL * ROWS, 256), jnp.float32),
            pltpu.VMEM((HEADS_LOCAL * ROWS, 128), jnp.float32),
            pltpu.VMEM((MICRO, HEADS_LOCAL, ROWS, HEAD_DIM), jnp.bfloat16),
            pltpu.VMEM((MICRO, 1, 128), jnp.float32),
            pltpu.VMEM((MICRO, N_HEAD, 1, 128), jnp.float32),
            dma((MICRO, 3)),
            dma(z_shape),
            dma(z_shape),
            dma(s_shape),
            dma(s_shape),
            dma((MICRO,)),
            dma((MICRO,)),
            dma((MICRO, HEADS_LOCAL)),
            dma((MICRO, HEADS_LOCAL)),
            dma((MICRO, N_HEAD)),
            dma((MICRO, N_HEAD)),
        ],
        compiler_params=pltpu.CompilerParams(
            collective_id=0, has_side_effects=True, vmem_limit_bytes=48 * 1024 * 1024
        ),
        name="attend_two_layers",
    )(block_order, doc_lengths, queries, keys, values)


def solution(mesh):
    placed = (
        P("segment", None, "dc", "head"),
        P("segment", None, "dc", "head"),
        P("segment", None, "dc", "head"),
        P(),
        P(),
    )
    return jax.shard_map(
        on_device,
        mesh=mesh,
        in_specs=placed,
        out_specs=P("segment", None, "dc", "head"),
        check_vma=False,
    )
```

time: 303 us -> 59.8 us (0.20)
  the two profiles are of different devices: /device:TPU:66 before, /device:TPU:2 now
where the time goes in v1:
time: 59.8 us; the launch traced here: 59.5 us
  Pallas kernels  55 us (92%)
  local copies, waits for them, and re-layouts  4.53 us (8%)
    pallas_call x1, Pallas kernels, on_device(): pl.pallas_call(kernel, out_shape=jax.ShapeDtypeStruct(queries.shape, jnp....  55 us
    unnamed x11, local copies, waits for them, and re-layouts  4.53 us

profile of v1, /device:TPU:2, one launch (start us, length us, event | category | flops | bytes accessed | tf_op | source)
XLA Modules:
  0.0 59.5 jit_solution(2643092762257770608)
XLA Ops:
  0.0 0.0 copy-start
  0.0 0.9 %copy-done = bf16[1,2,64,1024]{3,2,1,0:T(8,128)(2,1)S(1)} copy-done((bf16[1,2,64,1024]{3,2,1,0:T(8,128)(2,1)S(1)}, bf16[1,2,64,1024]{3,2,1,0:T(8,128)(2,1)}, u32[]{:S(2)}) %copy-start) | copy-done | bytes 262168
  1.0 0.0 copy-start.1
  1.0 0.8 %copy-done.1 = bf16[1,2,64,128]{3,2,1,0:T(8,128)(2,1)S(1)} copy-done((bf16[1,2,64,128]{3,2,1,0:T(8,128)(2,1)S(1)}, bf16[1,2,64,128]{3,2,1,0:T(8,128)(2,1)}, u32[]{:S(2)}) %copy-start.1) | copy-done | bytes 32792
  1.7 0.0 copy-start.2
  1.7 0.8 %copy-done.2 = bf16[1,2,64,128]{3,2,1,0:T(8,128)(2,1)S(1)} copy-done((bf16[1,2,64,128]{3,2,1,0:T(8,128)(2,1)S(1)}, bf16[1,2,64,128]{3,2,1,0:T(8,128)(2,1)}, u32[]{:S(2)}) %copy-start.2) | copy-done | bytes 32792
  2.5 0.0 copy-start.3
  2.5 0.7 %copy-done.3 = s32[2,64]{1,0:T(2,128)S(1)} copy-done((s32[2,64]{1,0:T(2,128)S(1)}, s32[2,64]{1,0:T(2,128)}, u32[]{:S(2)}) %copy-start.3) | copy-done | bytes 536
  3.1 0.0 copy-start.4
  3.1 0.7 %copy-done.4 = s32[2,16]{1,0:T(2,128)S(1)} copy-done((s32[2,16]{1,0:T(2,128)S(1)}, s32[2,16]{1,0:T(2,128)}, u32[]{:S(2)}) %copy-start.4) | copy-done | bytes 152
  3.8 55.0 %attend_two_layers.1 = bf16[1,2,64,1024]{3,2,1,0:T(8,128)(2,1)S(1)} custom-call(s32[2,64]{1,0:T(2,128)S(1)} %copy-done.3, s32[2,16]{1,0:T(2,128)S(1)} %copy-done.4, bf16[1,2,64,1024]{3,2,1,0:T(8,128)(2,1)S(1)} %copy-done, bf16[1,2,64,128]{3,2,1,0:T(8,128)(2,1)S(1)} %copy-done.1, bf16[1,2,64,128]{3,2,1,0:T(8,128)(2,1)S(1)} %copy-done.2), custom_call_target="tpu_custom_call" | custom-call | tf_op jit(solution)/shard_map/attend_two_layers/pallas_call | solution.py:413
  58.8 0.7 %copy.7 = bf16[1,2,64,1024]{3,2,1,0:T(8,128)(2,1)} copy(bf16[1,2,64,1024]{3,2,1,0:T(8,128)(2,1)S(1)} %attend_two_layers.1) | data formatting | bytes 524288
Async XLA Ops:
  0.0 0.9 %copy-start = (bf16[1,2,64,1024]{3,2,1,0:T(8,128)(2,1)S(1)}, bf16[1,2,64,1024]{3,2,1,0:T(8,128)(2,1)}, u32[]{:S(2)}) copy-start(bf16[1,2,64,1024]{3,2,1,0:T(8,128)(2,1)} %q_hbm.1) | copy-start | bytes 786436
  1.0 0.8 %copy-start.1 = (bf16[1,2,64,128]{3,2,1,0:T(8,128)(2,1)S(1)}, bf16[1,2,64,128]{3,2,1,0:T(8,128)(2,1)}, u32[]{:S(2)}) copy-start(bf16[1,2,64,128]{3,2,1,0:T(8,128)(2,1)} %k_hbm.1) | copy-start | bytes 98308
  1.7 0.8 %copy-start.2 = (bf16[1,2,64,128]{3,2,1,0:T(8,128)(2,1)S(1)}, bf16[1,2,64,128]{3,2,1,0:T(8,128)(2,1)}, u32[]{:S(2)}) copy-start(bf16[1,2,64,128]{3,2,1,0:T(8,128)(2,1)} %v_hbm.1) | copy-start | bytes 98308
  2.5 0.7 %copy-start.3 = (s32[2,64]{1,0:T(2,128)S(1)}, s32[2,64]{1,0:T(2,128)}, u32[]{:S(2)}) copy-start(s32[2,64]{1,0:T(2,128)} %order_ref.1) | copy-start | bytes 1540
  3.1 0.7 %copy-start.4 = (s32[2,16]{1,0:T(2,128)S(1)}, s32[2,16]{1,0:T(2,128)}, u32[]{:S(2)}) copy-start(s32[2,16]{1,0:T(2,128)} %lengths_ref.1) | copy-start | bytes 388

commit v2 on v1

v2 whole, which is shorter than its diff:
```python
import math

import jax
import jax.numpy as jnp
from jax import lax
from jax.experimental import pallas as pl
from jax.experimental.pallas import tpu as pltpu
from jax.sharding import PartitionSpec as P

HEAD_DIM = 128
BLOCK = 32
MICRO = 2
DOCS = 16
HEADS_LOCAL = 8
N_HEAD = 8
ROWS = 64
FEATURES = 8192
NZ = 8
FAR = NZ // 2
HIDDEN = -1e30
MESH = pl.DeviceIdType.MESH
EXP_SCALE = math.log2(math.e) / math.sqrt(HEAD_DIM)
GROUP_ROWS = 256


def start_rank(head):
    if isinstance(head, int):
        return 2 * head - 1 if 1 <= head <= N_HEAD // 2 else 2 * ((N_HEAD - head) % N_HEAD)
    return jnp.where(
        (head >= 1) & (head <= N_HEAD // 2), 2 * head - 1, 2 * ((N_HEAD - head) % N_HEAD)
    )


def kernel(
    order_hbm,
    lengths_hbm,
    q_hbm,
    k_hbm,
    v_hbm,
    o_ref,
    order_ref,
    lengths_ref,
    q_ref,
    buf,
    key_mask,
    query_mask,
    qx,
    acc,
    peak,
    att,
    ss_out,
    ss_in,
    load_sem,
    small_sem,
    z_send,
    z_recv,
    x_send,
    x_recv,
    s_send,
    s_recv,
    a_send,
    a_recv,
    n_send,
    n_recv,
    x_in,
    s_in,
    seg_in,
    y_in,
    y_all,
):
    seg = lax.axis_index("segment")
    dc = lax.axis_index("dc")
    head = lax.axis_index("head")
    core = dc % 2
    z = (dc // 2) % NZ
    xh = dc // (2 * NZ)
    half = z // FAR
    rank = start_rank(head)

    def place(x_hi, z_at, core_at):
        return (x_hi * NZ + z_at) * 2 + core_at

    sibling = (seg, place(xh, z, 1 - core), head)
    x_peer = (seg, place(1 - xh, z, core), head)

    def z_peer(z_at):
        return (seg, place(xh, z_at, core), head)

    def tell(sem, device):
        pl.semaphore_signal(sem, inc=1, device_id=device, device_id_type=MESH)

    small = (
        pltpu.make_async_copy(order_hbm, order_ref, small_sem.at[0]),
        pltpu.make_async_copy(lengths_hbm, lengths_ref, small_sem.at[1]),
    )
    loads = []
    for m in range(MICRO):
        mine = buf.at[m, core, z, xh]
        loads.append(
            (
                pltpu.make_async_copy(k_hbm.at[0, m], mine.at[0], load_sem.at[m, 0]),
                pltpu.make_async_copy(v_hbm.at[0, m], mine.at[1], load_sem.at[m, 1]),
                pltpu.make_async_copy(q_hbm.at[0, m], q_ref.at[m], load_sem.at[m, 2]),
            )
        )
    for m in range(MICRO):
        loads[m][0].start()
        loads[m][1].start()
    for copy in small:
        copy.start()
    for m in range(MICRO):
        loads[m][2].start()

    barrier = pltpu.get_barrier_semaphore()
    for z_at in range(NZ):
        @pl.when(z_at > z)
        def _():
            tell(barrier, z_peer(z_at))

    @pl.when(xh == 0)
    def _():
        tell(barrier, x_peer)

    @pl.when(core == 1)
    def _():
        tell(barrier, sibling)

    @pl.when(seg == 0)
    def _():
        tell(barrier, (1, dc, head))
        for h in range(N_HEAD):
            @pl.when(start_rank(h) > rank)
            def _():
                tell(barrier, (0, dc, h))

    greetings = z + xh + (1 - core) + seg + (1 - seg) * rank

    @pl.when(greetings > 0)
    def _():
        pl.semaphore_wait(barrier, greetings)

    @pl.when(xh == 1)
    def _():
        tell(x_in, x_peer)

    @pl.when(core == 0)
    def _():
        tell(s_in, sibling)

    @pl.when(seg == 1)
    def _():
        tell(seg_in, (0, dc, head))

    def z_send_copy(m, z_at):
        block = buf.at[m, core, z, xh]
        return pltpu.make_async_remote_copy(
            src_ref=block,
            dst_ref=block,
            send_sem=z_send.at[m, z_at],
            recv_sem=z_recv.at[m, z],
            device_id=z_peer(z_at),
            device_id_type=MESH,
        )

    def z_arrival(m, z_at):
        block = buf.at[m, core, z_at, xh]
        return pltpu.make_async_remote_copy(
            src_ref=block,
            dst_ref=block,
            send_sem=z_send.at[m, z_at],
            recv_sem=z_recv.at[m, z_at],
            device_id=z_peer(z_at),
            device_id_type=MESH,
        )

    def x_copy(m, z_at, x_at):
        block = buf.at[m, core, z_at, x_at]
        return pltpu.make_async_remote_copy(
            src_ref=block,
            dst_ref=block,
            send_sem=x_send.at[m, z_at],
            recv_sem=x_recv.at[m, z_at],
            device_id=x_peer,
            device_id_type=MESH,
        )

    def s_copy(m, z_at, core_at):
        block = buf.at[m, core_at, z_at]
        return pltpu.make_async_remote_copy(
            src_ref=block,
            dst_ref=block,
            send_sem=s_send.at[m, z_at],
            recv_sem=s_recv.at[m, z_at],
            device_id=sibling,
            device_id_type=MESH,
        )

    def near(i):
        return half * FAR + (z + i) % FAR

    def far(i):
        return (1 - half) * FAR + (z + i) % FAR

    def pass_z(m, z_at):
        z_arrival(m, z_at).wait_recv()

        @pl.when(z_at > z)
        def _():
            z_send_copy(m, z_at).start()

        x_copy(m, z_at, xh).start()

    def pass_x(m, z_at):
        x_copy(m, z_at, 1 - xh).wait_recv()
        s_copy(m, z_at, core).start()

    def wait_s(m, z_at):
        s_copy(m, z_at, 1 - core).wait_recv()

    def finish_sends(m):
        for z_at in range(NZ):
            @pl.when(z_at != z)
            def _():
                z_send_copy(m, z_at).wait_send()
            x_copy(m, z_at, xh).wait_send()
            s_copy(m, z_at, core).wait_send()

    def build_masks(m):
        lane = lax.broadcasted_iota(jnp.int32, (1, 128), 1)
        none = jnp.int32(1 << 20)
        low = jnp.full((1, 128), none, jnp.int32)
        high = jnp.zeros((1, 128), jnp.int32)
        run = jnp.int32(0)
        for d in range(DOCS):
            low = jnp.where(lane == d, run, low)
            run = run + lengths_ref[m, d]
            high = jnp.where(lane == d, run, high)
        for half in range(2):
            first = order_ref[m, dc * 2 + half] * BLOCK
            low = jnp.where(lane == DOCS + half, first + BLOCK, low)
            high = jnp.where(lane == DOCS + half, none, high)
            fine = (lane >= 32 + 32 * half) & (lane < 64 + 32 * half)
            low = jnp.where(fine, first + lane - (32 + 32 * half), low)
            high = jnp.where(fine, first + lane - (31 + 32 * half), high)
        high_q = jnp.where(lane < DOCS, high, none)
        row = lax.broadcasted_iota(jnp.int32, (BLOCK, 128), 0)
        for half in range(2):
            pos = order_ref[m, dc * 2 + half] * BLOCK + row
            hidden = (pos < low) | (pos >= high_q)
            query_mask[m, half * BLOCK : (half + 1) * BLOCK, :] = jnp.where(
                hidden, HIDDEN, 0.0
            ).astype(jnp.bfloat16)

        def one_z(z_at, carry):
            for c_at in range(2):
                for x_at in range(2):
                    for half in range(2):
                        number = place(x_at, z_at, c_at) * 2 + half
                        pos = order_ref[m, number] * BLOCK + row
                        inside = (pos >= low) & (pos < high)
                        key_mask[
                            m, z_at, c_at, x_at, half * BLOCK : (half + 1) * BLOCK, :
                        ] = jnp.where(inside, 1.0, 0.0).astype(jnp.bfloat16)
            return carry

        lax.fori_loop(0, NZ, one_z, 0)

    def start_rows(m):
        acc[m] = jnp.zeros((HEADS_LOCAL * ROWS, 256), jnp.float32)
        peak[m] = jnp.full((HEADS_LOCAL * ROWS, 128), HIDDEN, jnp.float32)

    def fold(m, z_list, first, count):
        keys, values = [], []
        for z_at in z_list:
            k = buf[m, :, z_at, :, 0].reshape(256, HEAD_DIM)
            v = buf[m, :, z_at, :, 1].reshape(256, HEAD_DIM)
            b = key_mask[m, z_at].reshape(256, 128)
            keys.append(jnp.concatenate([k, b], axis=1))
            values.append(jnp.concatenate([v, jnp.ones_like(v)], axis=1))
        kx = jnp.concatenate(keys, axis=0)
        vx = jnp.concatenate(values, axis=0)
        for start in range(first, first + count, GROUP_ROWS):
            rows = slice(start, start + GROUP_ROWS)
            scores = lax.dot_general(
                qx[m, rows, :], kx, (((1,), (1,)), ((), ())), preferred_element_type=jnp.float32
            )
            old = peak[m, rows, :]
            new = jnp.maximum(old, jnp.max(scores, axis=1, keepdims=True))
            peak[m, rows, :] = new
            weights = jnp.exp2((scores - new[:, :1]) * EXP_SCALE).astype(jnp.bfloat16)
            fade = jnp.exp2((old - new) * EXP_SCALE)
            acc[m, rows, :] = acc[m, rows, :] * jnp.concatenate([fade, fade], axis=1) + jnp.dot(
                weights, vx, preferred_element_type=jnp.float32
            )

    def finished(m, h):
        rows = slice(h * ROWS, (h + 1) * ROWS)
        out = (acc[m, rows, :HEAD_DIM] / acc[m, rows, HEAD_DIM:]).astype(jnp.bfloat16)
        o_ref[0, m, :, h * HEAD_DIM : (h + 1) * HEAD_DIM] = out
        return out

    def a_copy(m, h):
        return pltpu.make_async_remote_copy(
            src_ref=att.at[m, h],
            dst_ref=att.at[m, h],
            send_sem=a_send.at[m, h],
            recv_sem=a_recv.at[m, h],
            device_id=(1, dc, head),
            device_id_type=MESH,
        )

    def n_copy(m, h):
        return pltpu.make_async_remote_copy(
            src_ref=ss_out.at[m],
            dst_ref=ss_in.at[m, head],
            send_sem=n_send.at[m, h],
            recv_sem=n_recv.at[m, head],
            device_id=(1, dc, h),
            device_id_type=MESH,
        )

    def n_arrival(m, h):
        return pltpu.make_async_remote_copy(
            src_ref=ss_out.at[m],
            dst_ref=ss_in.at[m, h],
            send_sem=n_send.at[m, h],
            recv_sem=n_recv.at[m, h],
            device_id=(0, dc, h),
            device_id_type=MESH,
        )

    def stage_query(m, h, value):
        rows = slice(h * ROWS, (h + 1) * ROWS)
        qx[m, rows, :HEAD_DIM] = value
        qx[m, rows, HEAD_DIM:] = query_mask[m]

    def hand_over(m):
        squares = jnp.zeros((ROWS, HEAD_DIM), jnp.float32)
        for h in range(HEADS_LOCAL):
            out = finished(m, h)
            att[m, h] = out
            a_copy(m, h).start()
            wide = out.astype(jnp.float32)
            squares = squares + wide * wide
        ss_out[m, :, :ROWS] = jnp.sum(jnp.transpose(squares), axis=0, keepdims=True)
        for h in range(N_HEAD):
            n_copy(m, h).start()

    def fold_two(m, z_a, z_b):
        wait_s(m, z_a)
        wait_s(m, z_b)
        fold(m, (z_a, z_b), 0, HEADS_LOCAL * ROWS)

    for m in range(MICRO):
        loads[m][0].wait()
        loads[m][1].wait()
        for z_at in range(NZ):
            @pl.when(z_at < z)
            def _():
                z_send_copy(m, z_at).start()
    for copy in small:
        copy.wait()
    for m in range(MICRO):
        build_masks(m)
        start_rows(m)
        loads[m][2].wait()

    @pl.when(seg == 0)
    def _():
        for m in range(MICRO):
            for h in range(HEADS_LOCAL):
                stage_query(m, h, q_ref[m, :, h * HEAD_DIM : (h + 1) * HEAD_DIM])
        for h in range(N_HEAD):
            @pl.when(start_rank(h) < rank)
            def _():
                tell(y_in, (0, dc, h))

    @pl.when(xh == 0)
    def _():
        pl.semaphore_wait(x_in, 1)

    @pl.when(core == 1)
    def _():
        pl.semaphore_wait(s_in, 1)

    for m in range(MICRO):
        x_copy(m, z, xh).start()
    for i in range(1, FAR):
        for m in range(MICRO):
            pass_z(m, near(i))
    for i in range(FAR - 1):
        for m in range(MICRO):
            pass_x(m, near(i))

    @pl.when(seg == 0)
    def _():
        pl.semaphore_wait(seg_in, 1)

        @pl.when(rank < N_HEAD - 1)
        def _():
            pl.semaphore_wait(y_in, N_HEAD - 1 - rank)

        for h in range(N_HEAD):
            @pl.when(head != h)
            def _():
                tell(y_all, (0, dc, h))

    for i in range(FAR):
        pass_z(0, far(i))
    for m in range(MICRO):
        pass_x(m, near(FAR - 1))
    for i in range(FAR):
        pass_z(1, far(i))

    @pl.when(seg == 0)
    def _():
        fold_two(0, near(0), near(1))
        fold_two(0, near(2), near(3))

    for i in range(FAR):
        pass_x(0, far(i))

    @pl.when(seg == 0)
    def _():
        fold_two(1, near(0), near(1))
        fold_two(1, near(2), near(3))
        fold_two(0, far(0), far(1))
        fold_two(0, far(2), far(3))
        pl.semaphore_wait(y_all, N_HEAD - 1)
        hand_over(0)

    for i in range(FAR):
        pass_x(1, far(i))

    @pl.when(seg == 0)
    def _():
        fold_two(1, far(0), far(1))
        fold_two(1, far(2), far(3))
        hand_over(1)
        for m in range(MICRO):
            for h in range(HEADS_LOCAL):
                a_copy(m, h).wait_send()
                n_copy(m, h).wait_send()

    @pl.when(seg == 1)
    def _():
        for m in range(MICRO):
            for z_at in range(NZ):
                wait_s(m, z_at)
        for m in range(MICRO):
            for h in range(N_HEAD):
                n_arrival(m, h).wait_recv()
            total = ss_in[m, 0]
            for h in range(1, N_HEAD):
                total = total + ss_in[m, h]
            wide_total = jnp.broadcast_to(total[:, :ROWS], (HEAD_DIM, ROWS))
            norm = lax.rsqrt(jnp.transpose(wide_total) / FEATURES + 1e-05)
            per_group = GROUP_ROWS // ROWS
            for group in range(HEADS_LOCAL // per_group):
                for h in range(group * per_group, (group + 1) * per_group):
                    a_copy(m, h).wait_recv()
                    lifted = (
                        q_ref[m, :, h * HEAD_DIM : (h + 1) * HEAD_DIM].astype(jnp.float32)
                        + att[m, h].astype(jnp.float32) * norm
                    )
                    stage_query(m, h, lifted.astype(jnp.bfloat16))
                for pair in range(FAR):
                    fold(m, (2 * pair, 2 * pair + 1), group * GROUP_ROWS, GROUP_ROWS)
                for h in range(group * per_group, (group + 1) * per_group):
                    finished(m, h)

    for m in range(MICRO):
        finish_sends(m)


def on_device(queries, keys, values, block_order, doc_lengths):
    dma = pltpu.SemaphoreType.DMA
    regular = pltpu.SemaphoreType.REGULAR
    rows = HEADS_LOCAL * ROWS
    return pl.pallas_call(
        kernel,
        out_shape=jax.ShapeDtypeStruct(queries.shape, jnp.bfloat16),
        in_specs=[pl.BlockSpec(memory_space=pltpu.HBM)] * 5,
        out_specs=pl.BlockSpec(memory_space=pltpu.VMEM),
        scratch_shapes=[
            pltpu.SMEM((MICRO, 64), jnp.int32),
            pltpu.SMEM((MICRO, DOCS), jnp.int32),
            pltpu.VMEM((MICRO, ROWS, HEADS_LOCAL * HEAD_DIM), jnp.bfloat16),
            pltpu.VMEM((MICRO, 2, NZ, 2, 2, ROWS, HEAD_DIM), jnp.bfloat16),
            pltpu.VMEM((MICRO, NZ, 2, 2, ROWS, 128), jnp.bfloat16),
            pltpu.VMEM((MICRO, ROWS, 128), jnp.bfloat16),
            pltpu.VMEM((MICRO, rows, 256), jnp.bfloat16),
            pltpu.VMEM((MICRO, rows, 256), jnp.float32),
            pltpu.VMEM((MICRO, rows, 128), jnp.float32),
            pltpu.VMEM((MICRO, HEADS_LOCAL, ROWS, HEAD_DIM), jnp.bfloat16),
            pltpu.VMEM((MICRO, 1, 128), jnp.float32),
            pltpu.VMEM((MICRO, N_HEAD, 1, 128), jnp.float32),
            dma((MICRO, 3)),
            dma((2,)),
            dma((MICRO, NZ)),
            dma((MICRO, NZ)),
            dma((MICRO, NZ)),
            dma((MICRO, NZ)),
            dma((MICRO, NZ)),
            dma((MICRO, NZ)),
            dma((MICRO, HEADS_LOCAL)),
            dma((MICRO, HEADS_LOCAL)),
            dma((MICRO, N_HEAD)),
            dma((MICRO, N_HEAD)),
            regular,
            regular,
            regular,
            regular,
            regular,
        ],
        compiler_params=pltpu.CompilerParams(
            collective_id=0, has_side_effects=True, vmem_limit_bytes=48 * 1024 * 1024
        ),
        name="attend_two_layers",
    )(block_order, doc_lengths, queries, keys, values)


def solution(mesh):
    placed = (
        P("segment", None, "dc", "head"),
        P("segment", None, "dc", "head"),
        P("segment", None, "dc", "head"),
        P(),
        P(),
    )
    return jax.shard_map(
        on_device,
        mesh=mesh,
        in_specs=placed,
        out_specs=P("segment", None, "dc", "head"),
        check_vma=False,
    )
```

time: 59.8 us -> 54.4 us (0.910)
  the two profiles are of different devices: /device:TPU:2 before, /device:TPU:450 now
where the time goes in v2:
time: 54.4 us; the launch traced here: 54.1 us
  Pallas kernels  49.5 us (91%)
  local copies, waits for them, and re-layouts  4.53 us (8%)
    pallas_call x1, Pallas kernels, on_device(): pl.pallas_call(kernel, out_shape=jax.ShapeDtypeStruct(queries.shape, jnp....  49.5 us
    unnamed x11, local copies, waits for them, and re-layouts  4.53 us

profile of v2, /device:TPU:450, one launch (start us, length us, event | category | flops | bytes accessed | tf_op | source)
XLA Modules:
  0.0 54.1 jit_solution(11588864039927293729)
XLA Ops:
  0.0 0.0 copy-start
  0.0 0.9 %copy-done = bf16[1,2,64,1024]{3,2,1,0:T(8,128)(2,1)S(1)} copy-done((bf16[1,2,64,1024]{3,2,1,0:T(8,128)(2,1)S(1)}, bf16[1,2,64,1024]{3,2,1,0:T(8,128)(2,1)}, u32[]{:S(2)}) %copy-start) | copy-done | bytes 262168
  1.0 0.0 copy-start.1
  1.0 0.8 %copy-done.1 = bf16[1,2,64,128]{3,2,1,0:T(8,128)(2,1)S(1)} copy-done((bf16[1,2,64,128]{3,2,1,0:T(8,128)(2,1)S(1)}, bf16[1,2,64,128]{3,2,1,0:T(8,128)(2,1)}, u32[]{:S(2)}) %copy-start.1) | copy-done | bytes 32792
  1.7 0.0 copy-start.2
  1.7 0.8 %copy-done.2 = bf16[1,2,64,128]{3,2,1,0:T(8,128)(2,1)S(1)} copy-done((bf16[1,2,64,128]{3,2,1,0:T(8,128)(2,1)S(1)}, bf16[1,2,64,128]{3,2,1,0:T(8,128)(2,1)}, u32[]{:S(2)}) %copy-start.2) | copy-done | bytes 32792
  2.5 0.0 copy-start.3
  2.5 0.7 %copy-done.3 = s32[2,64]{1,0:T(2,128)S(1)} copy-done((s32[2,64]{1,0:T(2,128)S(1)}, s32[2,64]{1,0:T(2,128)}, u32[]{:S(2)}) %copy-start.3) | copy-done | bytes 536
  3.1 0.0 copy-start.4
  3.1 0.7 %copy-done.4 = s32[2,16]{1,0:T(2,128)S(1)} copy-done((s32[2,16]{1,0:T(2,128)S(1)}, s32[2,16]{1,0:T(2,128)}, u32[]{:S(2)}) %copy-start.4) | copy-done | bytes 152
  3.8 49.5 %attend_two_layers.1 = bf16[1,2,64,1024]{3,2,1,0:T(8,128)(2,1)S(1)} custom-call(s32[2,64]{1,0:T(2,128)S(1)} %copy-done.3, s32[2,16]{1,0:T(2,128)S(1)} %copy-done.4, bf16[1,2,64,1024]{3,2,1,0:T(8,128)(2,1)S(1)} %copy-done, bf16[1,2,64,128]{3,2,1,0:T(8,128)(2,1)S(1)} %copy-done.1, bf16[1,2,64,128]{3,2,1,0:T(8,128)(2,1)S(1)} %copy-done.2), custom_call_target="tpu_custom_call" | custom-call | tf_op jit(solution)/shard_map/attend_two_layers/pallas_call | solution.py:480
  53.4 0.7 %copy.7 = bf16[1,2,64,1024]{3,2,1,0:T(8,128)(2,1)} copy(bf16[1,2,64,1024]{3,2,1,0:T(8,128)(2,1)S(1)} %attend_two_layers.1) | data formatting | bytes 524288
Async XLA Ops:
  0.0 0.9 %copy-start = (bf16[1,2,64,1024]{3,2,1,0:T(8,128)(2,1)S(1)}, bf16[1,2,64,1024]{3,2,1,0:T(8,128)(2,1)}, u32[]{:S(2)}) copy-start(bf16[1,2,64,1024]{3,2,1,0:T(8,128)(2,1)} %q_hbm.1) | copy-start | bytes 786436
  1.0 0.8 %copy-start.1 = (bf16[1,2,64,128]{3,2,1,0:T(8,128)(2,1)S(1)}, bf16[1,2,64,128]{3,2,1,0:T(8,128)(2,1)}, u32[]{:S(2)}) copy-start(bf16[1,2,64,128]{3,2,1,0:T(8,128)(2,1)} %k_hbm.1) | copy-start | bytes 98308
  1.7 0.8 %copy-start.2 = (bf16[1,2,64,128]{3,2,1,0:T(8,128)(2,1)S(1)}, bf16[1,2,64,128]{3,2,1,0:T(8,128)(2,1)}, u32[]{:S(2)}) copy-start(bf16[1,2,64,128]{3,2,1,0:T(8,128)(2,1)} %v_hbm.1) | copy-start | bytes 98308
  2.5 0.7 %copy-start.3 = (s32[2,64]{1,0:T(2,128)S(1)}, s32[2,64]{1,0:T(2,128)}, u32[]{:S(2)}) copy-start(s32[2,64]{1,0:T(2,128)} %order_hbm.1) | copy-start | bytes 1540
  3.1 0.7 %copy-start.4 = (s32[2,16]{1,0:T(2,128)S(1)}, s32[2,16]{1,0:T(2,128)}, u32[]{:S(2)}) copy-start(s32[2,16]{1,0:T(2,128)} %lengths_hbm.1) | copy-start | bytes 388

commit v3 on v2

--- a/solution.py
+++ b/solution.py
@@ -62,6 +62,7 @@
     a_recv,
     n_send,
     n_recv,
+    z_in,
     x_in,
     s_in,
     seg_in,
@@ -139,6 +140,11 @@
     def _():
         pl.semaphore_wait(barrier, greetings)
 
+    for z_at in range(NZ):
+        @pl.when(z_at < z)
+        def _():
+            tell(z_in.at[z], z_peer(z_at))
+
     @pl.when(xh == 1)
     def _():
         tell(x_in, x_peer)
@@ -150,6 +156,13 @@
     @pl.when(seg == 1)
     def _():
         tell(seg_in, (0, dc, head))
+
+    @pl.when(seg == 0)
+    def _():
+        for h in range(N_HEAD):
+            @pl.when(start_rank(h) < rank)
+            def _():
+                tell(y_in, (0, dc, h))
 
     def z_send_copy(m, z_at):
         block = buf.at[m, core, z, xh]
@@ -203,11 +216,6 @@
 
     def pass_z(m, z_at):
         z_arrival(m, z_at).wait_recv()
-
-        @pl.when(z_at > z)
-        def _():
-            z_send_copy(m, z_at).start()
-
         x_copy(m, z_at, xh).start()
 
     def pass_x(m, z_at):
@@ -269,7 +277,7 @@
         acc[m] = jnp.zeros((HEADS_LOCAL * ROWS, 256), jnp.float32)
         peak[m] = jnp.full((HEADS_LOCAL * ROWS, 128), HIDDEN, jnp.float32)
 
-    def fold(m, z_list, first, count):
+    def gathered(m, z_list):
         keys, values = [], []
         for z_at in z_list:
             k = buf[m, :, z_at, :, 0].reshape(256, HEAD_DIM)
@@ -277,13 +285,18 @@
             b = key_mask[m, z_at].reshape(256, 128)
             keys.append(jnp.concatenate([k, b], axis=1))
             values.append(jnp.concatenate([v, jnp.ones_like(v)], axis=1))
-        kx = jnp.concatenate(keys, axis=0)
-        vx = jnp.concatenate(values, axis=0)
-        for start in range(first, first + count, GROUP_ROWS):
+        return jnp.concatenate(keys, axis=0), jnp.concatenate(values, axis=0)
+
+    def score(m, rows, kx):
+        return lax.dot_general(
+            qx[m, rows, :], kx, (((1,), (1,)), ((), ())), preferred_element_type=jnp.float32
+        )
+
+    def fold(m, z_list):
+        kx, vx = gathered(m, z_list)
+        for start in range(0, HEADS_LOCAL * ROWS, GROUP_ROWS):
             rows = slice(start, start + GROUP_ROWS)
-            scores = lax.dot_general(
-                qx[m, rows, :], kx, (((1,), (1,)), ((), ())), preferred_element_type=jnp.float32
-            )
+            scores = score(m, rows, kx)
             old = peak[m, rows, :]
             new = jnp.maximum(old, jnp.max(scores, axis=1, keepdims=True))
             peak[m, rows, :] = new
@@ -292,6 +305,14 @@
             acc[m, rows, :] = acc[m, rows, :] * jnp.concatenate([fade, fade], axis=1) + jnp.dot(
                 weights, vx, preferred_element_type=jnp.float32
             )
+
+    def fold_all(m, start):
+        kx, vx = gathered(m, range(NZ))
+        rows = slice(start, start + GROUP_ROWS)
+        scores = score(m, rows, kx)
+        top = jnp.max(scores, axis=1, keepdims=True)
+        weights = jnp.exp2((scores - top) * EXP_SCALE).astype(jnp.bfloat16)
+        acc[m, rows, :] = jnp.dot(weights, vx, preferred_element_type=jnp.float32)
 
     def finished(m, h):
         rows = slice(h * ROWS, (h + 1) * ROWS)
@@ -346,10 +367,20 @@
         for h in range(N_HEAD):
             n_copy(m, h).start()
 
-    def fold_two(m, z_a, z_b):
-        wait_s(m, z_a)
-        wait_s(m, z_b)
-        fold(m, (z_a, z_b), 0, HEADS_LOCAL * ROWS)
+    def fold_four(m, z_list):
+        for z_at in z_list:
+            wait_s(m, z_at)
+        fold(m, z_list)
+
+    def prepare(m):
+        build_masks(m)
+        loads[m][2].wait()
+
+        @pl.when(seg == 0)
+        def _():
+            start_rows(m)
+            for h in range(HEADS_LOCAL):
+                stage_query(m, h, q_ref[m, :, h * HEAD_DIM : (h + 1) * HEAD_DIM])
 
     for m in range(MICRO):
         loads[m][0].wait()
@@ -358,22 +389,16 @@
             @pl.when(z_at < z)
             def _():
                 z_send_copy(m, z_at).start()
+    for i in range(1, FAR):
+        @pl.when(near(i) > z)
+        def _():
+            pl.semaphore_wait(z_in.at[near(i)], 1)
+            for m in range(MICRO):
+                z_send_copy(m, near(i)).start()
+
     for copy in small:
         copy.wait()
-    for m in range(MICRO):
-        build_masks(m)
-        start_rows(m)
-        loads[m][2].wait()
-
-    @pl.when(seg == 0)
-    def _():
-        for m in range(MICRO):
-            for h in range(HEADS_LOCAL):
-                stage_query(m, h, q_ref[m, :, h * HEAD_DIM : (h + 1) * HEAD_DIM])
-        for h in range(N_HEAD):
-            @pl.when(start_rank(h) < rank)
-            def _():
-                tell(y_in, (0, dc, h))
+    prepare(0)
 
     @pl.when(xh == 0)
     def _():
@@ -385,9 +410,19 @@
 
     for m in range(MICRO):
         x_copy(m, z, xh).start()
+    prepare(1)
     for i in range(1, FAR):
         for m in range(MICRO):
             pass_z(m, near(i))
+
+    @pl.when(half == 0)
+    def _():
+        for i in range(FAR):
+            pl.semaphore_wait(z_in.at[far(i)], 1)
+            z_send_copy(0, far(i)).start()
+        for i in range(FAR):
+            z_send_copy(1, far(i)).start()
+
     for i in range(FAR - 1):
         for m in range(MICRO):
             pass_x(m, near(i))
@@ -412,30 +447,29 @@
     for i in range(FAR):
         pass_z(1, far(i))
 
+    nears = tuple(near(i) for i in range(FAR))
+    fars = tuple(far(i) for i in range(FAR))
+
     @pl.when(seg == 0)
     def _():
-        fold_two(0, near(0), near(1))
-        fold_two(0, near(2), near(3))
+        fold_four(0, nears)
 
     for i in range(FAR):
         pass_x(0, far(i))
 
     @pl.when(seg == 0)
     def _():
-        fold_two(1, near(0), near(1))
-        fold_two(1, near(2), near(3))
-        fold_two(0, far(0), far(1))
-        fold_two(0, far(2), far(3))
+        fold_four(0, fars)
         pl.semaphore_wait(y_all, N_HEAD - 1)
         hand_over(0)
+        fold_four(1, nears)
 
     for i in range(FAR):
         pass_x(1, far(i))
 
     @pl.when(seg == 0)
     def _():
-        fold_two(1, far(0), far(1))
-        fold_two(1, far(2), far(3))
+        fold_four(1, fars)
         hand_over(1)
         for m in range(MICRO):
             for h in range(HEADS_LOCAL):
@@ -464,8 +498,7 @@
                         + att[m, h].astype(jnp.float32) * norm
                     )
                     stage_query(m, h, lifted.astype(jnp.bfloat16))
-                for pair in range(FAR):
-                    fold(m, (2 * pair, 2 * pair + 1), group * GROUP_ROWS, GROUP_ROWS)
+                fold_all(m, group * GROUP_ROWS)
                 for h in range(group * per_group, (group + 1) * per_group):
                     finished(m, h)
 
@@ -507,6 +540,7 @@
             dma((MICRO, HEADS_LOCAL)),
             dma((MICRO, N_HEAD)),
             dma((MICRO, N_HEAD)),
+            pltpu.SemaphoreType.REGULAR((NZ,)),
             regular,
             regular,
             regular,
@@ -514,7 +548,7 @@
             regular,
         ],
         compiler_params=pltpu.CompilerParams(
-            collective_id=0, has_side_effects=True, vmem_limit_bytes=48 * 1024 * 1024
+            collective_id=0, has_side_effects=True, vmem_limit_bytes=62 * 1024 * 1024
         ),
         name="attend_two_layers",
     )(block_order, doc_lengths, queries, keys, values)

time: 54.4 us -> 46.5 us (0.85)
  the two profiles are of different devices: /device:TPU:450 before, /device:TPU:258 now
where the time goes in v3:
time: 46.5 us; the launch traced here: 46.3 us
  Pallas kernels  44.7 us (96%)
  local copies, waits for them, and re-layouts  1.67 us (4%)
    pallas_call x1, Pallas kernels, on_device(): pl.pallas_call(kernel, out_shape=jax.ShapeDtypeStruct(queries.shape, jnp....  44.7 us
    unnamed x1, local copies, waits for them, and re-layouts  1.67 us

profile of v3, /device:TPU:258, one launch (start us, length us, event | category | flops | bytes accessed | tf_op | source)
XLA Modules:
  0.0 46.3 jit_solution(13005264287160741310)
XLA Ops:
  0.0 44.7 %attend_two_layers.1 = bf16[1,2,64,1024]{3,2,1,0:T(8,128)(2,1)} custom-call(s32[2,64]{1,0:T(2,128)} %order_hbm.1, s32[2,16]{1,0:T(2,128)} %lengths_hbm.1, bf16[1,2,64,1024]{3,2,1,0:T(8,128)(2,1)} %q_hbm.1, bf16[1,2,64,128]{3,2,1,0:T(8,128)(2,1)} %k_hbm.1, bf16[1,2,64,128]{3,2,1,0:T(8,128)(2,1)} %v_hbm.1), custom_call_target="tpu_custom_call" | custom-call | tf_op jit(solution)/shard_map/attend_two_layers/pallas_call | solution.py:513
  44.7 1.7 %copy.7 = bf16[1,2,64,1024]{3,2,1,0:T(8,128)(2,1)} copy(bf16[1,2,64,1024]{3,2,1,0:T(8,128)(2,1)} %attend_two_layers.1) | data formatting | bytes 524288

commit v4 on v3

--- a/solution.py
+++ b/solution.py
@@ -292,33 +292,34 @@
             qx[m, rows, :], kx, (((1,), (1,)), ((), ())), preferred_element_type=jnp.float32
         )
 
+    groups = [
+        slice(start, start + GROUP_ROWS) for start in range(0, HEADS_LOCAL * ROWS, GROUP_ROWS)
+    ]
+
     def fold(m, z_list):
         kx, vx = gathered(m, z_list)
-        for start in range(0, HEADS_LOCAL * ROWS, GROUP_ROWS):
-            rows = slice(start, start + GROUP_ROWS)
-            scores = score(m, rows, kx)
+        scores = [score(m, rows, kx) for rows in groups]
+        for rows, one in zip(groups, scores):
             old = peak[m, rows, :]
-            new = jnp.maximum(old, jnp.max(scores, axis=1, keepdims=True))
+            new = jnp.maximum(old, jnp.max(one, axis=1, keepdims=True))
             peak[m, rows, :] = new
-            weights = jnp.exp2((scores - new[:, :1]) * EXP_SCALE).astype(jnp.bfloat16)
+            weights = jnp.exp2((one - new[:, :1]) * EXP_SCALE).astype(jnp.bfloat16)
             fade = jnp.exp2((old - new) * EXP_SCALE)
             acc[m, rows, :] = acc[m, rows, :] * jnp.concatenate([fade, fade], axis=1) + jnp.dot(
                 weights, vx, preferred_element_type=jnp.float32
             )
 
-    def fold_all(m, start):
-        kx, vx = gathered(m, range(NZ))
-        rows = slice(start, start + GROUP_ROWS)
-        scores = score(m, rows, kx)
+    def settle(m, vx, rows, scores):
         top = jnp.max(scores, axis=1, keepdims=True)
         weights = jnp.exp2((scores - top) * EXP_SCALE).astype(jnp.bfloat16)
         acc[m, rows, :] = jnp.dot(weights, vx, preferred_element_type=jnp.float32)
 
     def finished(m, h):
         rows = slice(h * ROWS, (h + 1) * ROWS)
-        out = (acc[m, rows, :HEAD_DIM] / acc[m, rows, HEAD_DIM:]).astype(jnp.bfloat16)
+        return (acc[m, rows, :HEAD_DIM] / acc[m, rows, HEAD_DIM:]).astype(jnp.bfloat16)
+
+    def put(m, h, out):
         o_ref[0, m, :, h * HEAD_DIM : (h + 1) * HEAD_DIM] = out
-        return out
 
     def a_copy(m, h):
         return pltpu.make_async_remote_copy(
@@ -360,12 +361,15 @@
         for h in range(HEADS_LOCAL):
             out = finished(m, h)
             att[m, h] = out
-            a_copy(m, h).start()
             wide = out.astype(jnp.float32)
             squares = squares + wide * wide
         ss_out[m, :, :ROWS] = jnp.sum(jnp.transpose(squares), axis=0, keepdims=True)
         for h in range(N_HEAD):
             n_copy(m, h).start()
+        for h in range(HEADS_LOCAL):
+            a_copy(m, h).start()
+        for h in range(HEADS_LOCAL):
+            put(m, h, att[m, h])
 
     def fold_four(m, z_list):
         for z_at in z_list:
@@ -489,18 +493,21 @@
                 total = total + ss_in[m, h]
             wide_total = jnp.broadcast_to(total[:, :ROWS], (HEAD_DIM, ROWS))
             norm = lax.rsqrt(jnp.transpose(wide_total) / FEATURES + 1e-05)
-            per_group = GROUP_ROWS // ROWS
-            for group in range(HEADS_LOCAL // per_group):
-                for h in range(group * per_group, (group + 1) * per_group):
+            kx, vx = gathered(m, range(NZ))
+            scores = []
+            for rows in groups:
+                for h in range(rows.start // ROWS, rows.stop // ROWS):
                     a_copy(m, h).wait_recv()
                     lifted = (
                         q_ref[m, :, h * HEAD_DIM : (h + 1) * HEAD_DIM].astype(jnp.float32)
                         + att[m, h].astype(jnp.float32) * norm
                     )
                     stage_query(m, h, lifted.astype(jnp.bfloat16))
-                fold_all(m, group * GROUP_ROWS)
-                for h in range(group * per_group, (group + 1) * per_group):
-                    finished(m, h)
+                scores.append(score(m, rows, kx))
+            for rows, one in zip(groups, scores):
+                settle(m, vx, rows, one)
+            for h in range(HEADS_LOCAL):
+                put(m, h, finished(m, h))
 
     for m in range(MICRO):
         finish_sends(m)
@@ -510,6 +517,10 @@
     dma = pltpu.SemaphoreType.DMA
     regular = pltpu.SemaphoreType.REGULAR
     rows = HEADS_LOCAL * ROWS
+    operands = [
+        pltpu.with_memory_space_constraint(one, pltpu.HBM)
+        for one in (block_order, doc_lengths, queries, keys, values)
+    ]
     return pl.pallas_call(
         kernel,
         out_shape=jax.ShapeDtypeStruct(queries.shape, jnp.bfloat16),
@@ -548,10 +559,10 @@
             regular,
         ],
         compiler_params=pltpu.CompilerParams(
-            collective_id=0, has_side_effects=True, vmem_limit_bytes=62 * 1024 * 1024
+            collective_id=0, has_side_effects=True, vmem_limit_bytes=48 * 1024 * 1024
         ),
         name="attend_two_layers",
-    )(block_order, doc_lengths, queries, keys, values)
+    )(*operands)
 
 
 def solution(mesh):

time: 46.5 us -> 43.1 us (0.927)
  Pallas kernels: 44.7 us -> 42.2 us
  local copies, waits for them, and re-layouts: 1.67 us -> 0.71 us
    pallas_call x1, Pallas kernels: 44.7 us -> 42.2 us  [on_device(): pl.pallas_call(kernel, out_shape=jax.ShapeDtypeStruct(queries.shape, jnp....]
    unnamed x1, local copies, waits for them, and re-layouts: 1.67 us -> 0.71 us
where the time goes in v4:
time: 43.1 us; the launch traced here: 43 us
  Pallas kernels  42.2 us (98%)
  local copies, waits for them, and re-layouts  0.71 us (2%)
    pallas_call x1, Pallas kernels, on_device(): pl.pallas_call(kernel, out_shape=jax.ShapeDtypeStruct(queries.shape, jnp....  42.2 us

profile of v4, /device:TPU:258, one launch (start us, length us, event | category | flops | bytes accessed | tf_op | source)
XLA Modules:
  0.0 43.0 jit_solution(2929748893953273081)
XLA Ops:
  0.0 42.2 %attend_two_layers.1 = bf16[1,2,64,1024]{3,2,1,0:T(8,128)(2,1)S(1)} custom-call(s32[2,64]{1,0:T(2,128)} %order_hbm.1, s32[2,16]{1,0:T(2,128)} %lengths_hbm.1, bf16[1,2,64,1024]{3,2,1,0:T(8,128)(2,1)} %q_hbm.1, bf16[1,2,64,128]{3,2,1,0:T(8,128)(2,1)} %k_hbm.1, bf16[1,2,64,128]{3,2,1,0:T(8,128)(2,1)} %v_hbm.1), custom_call_target="tpu_custom_call" | custom-call | tf_op jit(solution)/shard_map/attend_two_layers/pallas_call | solution.py:524
  42.2 0.7 %copy.7 = bf16[1,2,64,1024]{3,2,1,0:T(8,128)(2,1)} copy(bf16[1,2,64,1024]{3,2,1,0:T(8,128)(2,1)S(1)} %attend_two_layers.1) | data formatting | bytes 524288

commit v5 on v4

--- a/solution.py
+++ b/solution.py
@@ -54,6 +54,7 @@
     small_sem,
     z_send,
     z_recv,
+    r_send,
     x_send,
     x_recv,
     s_send,
@@ -76,6 +77,7 @@
     z = (dc // 2) % NZ
     xh = dc // (2 * NZ)
     half = z // FAR
+    side = (z % FAR) // 2
     rank = start_rank(head)
 
     def place(x_hi, z_at, core_at):
@@ -112,11 +114,27 @@
     for m in range(MICRO):
         loads[m][2].start()
 
+    def near(i):
+        return half * FAR + (z + i) % FAR
+
+    def far(i):
+        return (1 - half) * FAR + jnp.where(i < 2, 1 - side, side) * 2 + (z + i) % 2
+
+    def direct(i):
+        return (side == 0) | (i < 2)
+
+    def across(i):
+        return half * FAR + (1 - side) * 2 + i
+
     barrier = pltpu.get_barrier_semaphore()
-    for z_at in range(NZ):
-        @pl.when(z_at > z)
-        def _():
-            tell(barrier, z_peer(z_at))
+    for i in range(1, FAR):
+        @pl.when(near(i) > z)
+        def _():
+            tell(barrier, z_peer(near(i)))
+    for i in range(FAR):
+        @pl.when((far(i) > z) & direct(i))
+        def _():
+            tell(barrier, z_peer(far(i)))
 
     @pl.when(xh == 0)
     def _():
@@ -134,16 +152,20 @@
             def _():
                 tell(barrier, (0, dc, h))
 
-    greetings = z + xh + (1 - core) + seg + (1 - seg) * rank
+    greetings = z % FAR + half * (4 - 2 * side) + xh + (1 - core) + seg + (1 - seg) * rank
 
     @pl.when(greetings > 0)
     def _():
         pl.semaphore_wait(barrier, greetings)
 
-    for z_at in range(NZ):
-        @pl.when(z_at < z)
-        def _():
-            tell(z_in.at[z], z_peer(z_at))
+    for i in range(1, FAR):
+        @pl.when(near(i) < z)
+        def _():
+            tell(z_in.at[z], z_peer(near(i)))
+    for i in range(FAR):
+        @pl.when((far(i) < z) & direct(i))
+        def _():
+            tell(z_in.at[z], z_peer(far(i)))
 
     @pl.when(xh == 1)
     def _():
@@ -208,11 +230,29 @@
             device_id_type=MESH,
         )
 
-    def near(i):
-        return half * FAR + (z + i) % FAR
-
-    def far(i):
-        return (1 - half) * FAR + (z + i) % FAR
+    def relays():
+        return z % FAR == 1
+
+    def relay_copy(m, i, j):
+        block = buf.at[m, core, far(i), xh]
+        return pltpu.make_async_remote_copy(
+            src_ref=block,
+            dst_ref=block,
+            send_sem=r_send.at[m, i, j],
+            recv_sem=z_recv.at[m, far(i)],
+            device_id=z_peer(across(j)),
+            device_id_type=MESH,
+        )
+
+    def pass_far(m, i):
+        z_arrival(m, far(i)).wait_recv()
+        if i < 2:
+            @pl.when(relays())
+            def _():
+                for j in range(2):
+                    relay_copy(m, i, j).start()
+
+        x_copy(m, far(i), xh).start()
 
     def pass_z(m, z_at):
         z_arrival(m, z_at).wait_recv()
@@ -226,10 +266,20 @@
         s_copy(m, z_at, 1 - core).wait_recv()
 
     def finish_sends(m):
+        for i in range(1, FAR):
+            z_send_copy(m, near(i)).wait_send()
+        for i in range(FAR):
+            @pl.when(direct(i))
+            def _():
+                z_send_copy(m, far(i)).wait_send()
+
+        @pl.when(relays())
+        def _():
+            for i in range(2):
+                for j in range(2):
+                    relay_copy(m, i, j).wait_send()
+
         for z_at in range(NZ):
-            @pl.when(z_at != z)
-            def _():
-                z_send_copy(m, z_at).wait_send()
             x_copy(m, z_at, xh).wait_send()
             s_copy(m, z_at, core).wait_send()
 
@@ -389,11 +439,15 @@
     for m in range(MICRO):
         loads[m][0].wait()
         loads[m][1].wait()
-        for z_at in range(NZ):
-            @pl.when(z_at < z)
-            def _():
-                z_send_copy(m, z_at).start()
-    for i in range(1, FAR):
+        for i in range(FAR):
+            @pl.when((far(i) < z) & direct(i))
+            def _():
+                z_send_copy(m, far(i)).start()
+        for i in range(1, FAR):
+            @pl.when(near(i) < z)
+            def _():
+                z_send_copy(m, near(i)).start()
+    def answer_near(i):
         @pl.when(near(i) > z)
         def _():
             pl.semaphore_wait(z_in.at[near(i)], 1)
@@ -403,6 +457,8 @@
     for copy in small:
         copy.wait()
     prepare(0)
+    answer_near(1)
+    answer_near(2)
 
     @pl.when(xh == 0)
     def _():
@@ -414,6 +470,7 @@
 
     for m in range(MICRO):
         x_copy(m, z, xh).start()
+    answer_near(3)
     prepare(1)
     for i in range(1, FAR):
         for m in range(MICRO):
@@ -422,10 +479,14 @@
     @pl.when(half == 0)
     def _():
         for i in range(FAR):
-            pl.semaphore_wait(z_in.at[far(i)], 1)
-            z_send_copy(0, far(i)).start()
+            @pl.when(direct(i))
+            def _():
+                pl.semaphore_wait(z_in.at[far(i)], 1)
+                z_send_copy(0, far(i)).start()
         for i in range(FAR):
-            z_send_copy(1, far(i)).start()
+            @pl.when(direct(i))
+            def _():
+                z_send_copy(1, far(i)).start()
 
     for i in range(FAR - 1):
         for m in range(MICRO):
@@ -444,31 +505,50 @@
             def _():
                 tell(y_all, (0, dc, h))
 
-    for i in range(FAR):
-        pass_z(0, far(i))
+    nears = tuple(near(i) for i in range(FAR))
+    fars = tuple(far(i) for i in range(FAR))
+
+    @pl.when(side == 0)
+    def _():
+        for i in range(FAR):
+            pass_far(0, i)
+        for i in range(2):
+            pass_far(1, i)
+
+    @pl.when(side == 1)
+    def _():
+        for m in range(MICRO):
+            for i in range(2):
+                pass_far(m, i)
+        for i in range(2, FAR):
+            pass_far(0, i)
+
     for m in range(MICRO):
         pass_x(m, near(FAR - 1))
-    for i in range(FAR):
-        pass_z(1, far(i))
-
-    nears = tuple(near(i) for i in range(FAR))
-    fars = tuple(far(i) for i in range(FAR))
 
     @pl.when(seg == 0)
     def _():
         fold_four(0, nears)
 
+    for i in range(2, FAR):
+        pass_far(1, i)
     for i in range(FAR):
         pass_x(0, far(i))
 
     @pl.when(seg == 0)
     def _():
+        fold_four(1, nears)
         fold_four(0, fars)
+
+    for i in range(2):
+        pass_x(1, far(i))
+
+    @pl.when(seg == 0)
+    def _():
         pl.semaphore_wait(y_all, N_HEAD - 1)
         hand_over(0)
-        fold_four(1, nears)
-
-    for i in range(FAR):
+
+    for i in range(2, FAR):
         pass_x(1, far(i))
 
     @pl.when(seg == 0)
@@ -543,6 +623,7 @@
             dma((2,)),
             dma((MICRO, NZ)),
             dma((MICRO, NZ)),
+            dma((MICRO, 2, 2)),
             dma((MICRO, NZ)),
             dma((MICRO, NZ)),
             dma((MICRO, NZ)),

time: 43.1 us -> 41 us (0.951)
  the two profiles are of different devices: /device:TPU:258 before, /device:TPU:2 now
where the time goes in v5:
time: 41 us; the launch traced here: 40.9 us
  Pallas kernels  40.2 us (98%)
  local copies, waits for them, and re-layouts  0.71 us (2%)
    pallas_call x1, Pallas kernels, on_device(): pl.pallas_call(kernel, out_shape=jax.ShapeDtypeStruct(queries.shape, jnp....  40.2 us

profile of v5, /device:TPU:2, one launch (start us, length us, event | category | flops | bytes accessed | tf_op | source)
XLA Modules:
  0.0 40.9 jit_solution(11580496532852989938)
XLA Ops:
  0.0 40.2 %attend_two_layers.1 = bf16[1,2,64,1024]{3,2,1,0:T(8,128)(2,1)S(1)} custom-call(s32[2,64]{1,0:T(2,128)} %order_hbm.1, s32[2,16]{1,0:T(2,128)} %lengths_hbm.1, bf16[1,2,64,1024]{3,2,1,0:T(8,128)(2,1)} %q_hbm.1, bf16[1,2,64,128]{3,2,1,0:T(8,128)(2,1)} %k_hbm.1, bf16[1,2,64,128]{3,2,1,0:T(8,128)(2,1)} %v_hbm.1), custom_call_target="tpu_custom_call" | custom-call | tf_op jit(solution)/shard_map/attend_two_layers/pallas_call | solution.py:604
  40.2 0.7 %copy.7 = bf16[1,2,64,1024]{3,2,1,0:T(8,128)(2,1)} copy(bf16[1,2,64,1024]{3,2,1,0:T(8,128)(2,1)S(1)} %attend_two_layers.1) | data formatting | bytes 524288

commit v6 on v5

--- a/solution.py
+++ b/solution.py
@@ -21,6 +21,7 @@
 MESH = pl.DeviceIdType.MESH
 EXP_SCALE = math.log2(math.e) / math.sqrt(HEAD_DIM)
 GROUP_ROWS = 256
+WINDOW = 1024 // BLOCK + 1
 
 
 def start_rank(head):
@@ -50,8 +51,14 @@
     att,
     ss_out,
     ss_in,
+    inverse_v,
+    inverse,
+    k_win,
+    v_win,
+    b_win,
     load_sem,
     small_sem,
+    inverse_sem,
     z_send,
     z_recv,
     r_send,
@@ -100,19 +107,24 @@
     for m in range(MICRO):
         mine = buf.at[m, core, z, xh]
         loads.append(
-            (
-                pltpu.make_async_copy(k_hbm.at[0, m], mine.at[0], load_sem.at[m, 0]),
-                pltpu.make_async_copy(v_hbm.at[0, m], mine.at[1], load_sem.at[m, 1]),
-                pltpu.make_async_copy(q_hbm.at[0, m], q_ref.at[m], load_sem.at[m, 2]),
-            )
+            [
+                pltpu.make_async_copy(
+                    source.at[0, m, pl.ds(part * BLOCK, BLOCK)],
+                    mine.at[which, part],
+                    load_sem.at[m, which * 2 + part],
+                )
+                for which, source in enumerate((k_hbm, v_hbm))
+                for part in range(2)
+            ]
+            + [pltpu.make_async_copy(q_hbm.at[0, m], q_ref.at[m], load_sem.at[m, 4])]
         )
     for m in range(MICRO):
-        loads[m][0].start()
-        loads[m][1].start()
+        for one in loads[m][:4]:
+            one.start()
     for copy in small:
         copy.start()
     for m in range(MICRO):
-        loads[m][2].start()
+        loads[m][4].start()
 
     def near(i):
         return half * FAR + (z + i) % FAR
@@ -316,9 +328,7 @@
                         number = place(x_at, z_at, c_at) * 2 + half
                         pos = order_ref[m, number] * BLOCK + row
                         inside = (pos >= low) & (pos < high)
-                        key_mask[
-                            m, z_at, c_at, x_at, half * BLOCK : (half + 1) * BLOCK, :
-                        ] = jnp.where(inside, 1.0, 0.0).astype(jnp.bfloat16)
+                        key_mask[m, z_at, c_at, x_at, half] = jnp.where(inside, 1.0, 0.0).astype(jnp.bfloat16)
             return carry
 
         lax.fori_loop(0, NZ, one_z, 0)
@@ -421,6 +431,35 @@
         for h in range(HEADS_LOCAL):
             put(m, h, att[m, h])
 
+    def inverse_copy(m):
+        return pltpu.make_async_copy(inverse_v.at[m], inverse.at[m], inverse_sem.at[m])
+
+    def invert_order(m):
+        lane = lax.broadcasted_iota(jnp.int32, (1, 128), 1)
+        slot_block = jnp.zeros((1, 128), jnp.int32)
+        for number in range(64):
+            slot_block = jnp.where(lane == order_ref[m, number], number, slot_block)
+        inverse_v[m] = slot_block
+        inverse_copy(m).start()
+
+    def cut_windows(m):
+        for own in range(2):
+            base = jnp.maximum(order_ref[m, dc * 2 + own] - (WINDOW - 1), 0)
+
+            def one_block(j, carry, own=own, base=base):
+                number = inverse[m, 0, base + j]
+                c_at = (number >> 1) & 1
+                z_at = (number >> 2) & (NZ - 1)
+                x_at = number >> 5
+                h_at = number & 1
+                target = pl.ds(pl.multiple_of(j * BLOCK, BLOCK), BLOCK)
+                k_win[m, own, target, :] = buf[m, c_at, z_at, x_at, 0, h_at]
+                v_win[m, own, target, :] = buf[m, c_at, z_at, x_at, 1, h_at]
+                b_win[m, own, target, :] = key_mask[m, z_at, c_at, x_at, h_at]
+                return carry
+
+            lax.fori_loop(0, WINDOW, one_block, 0, unroll=3)
+
     def fold_four(m, z_list):
         for z_at in z_list:
             wait_s(m, z_at)
@@ -428,7 +467,11 @@
 
     def prepare(m):
         build_masks(m)
-        loads[m][2].wait()
+        loads[m][4].wait()
+
+        @pl.when(seg == 1)
+        def _():
+            invert_order(m)
 
         @pl.when(seg == 0)
         def _():
@@ -437,8 +480,8 @@
                 stage_query(m, h, q_ref[m, :, h * HEAD_DIM : (h + 1) * HEAD_DIM])
 
     for m in range(MICRO):
-        loads[m][0].wait()
-        loads[m][1].wait()
+        for one in loads[m][:4]:
+            one.wait()
         for i in range(FAR):
             @pl.when((far(i) < z) & direct(i))
             def _():
@@ -526,31 +569,33 @@
     for m in range(MICRO):
         pass_x(m, near(FAR - 1))
 
+    pass_far(1, 2)
+    pass_far(1, 3)
+    pass_x(0, far(0))
+    pass_x(0, far(1))
     @pl.when(seg == 0)
     def _():
         fold_four(0, nears)
 
-    for i in range(2, FAR):
-        pass_far(1, i)
-    for i in range(FAR):
-        pass_x(0, far(i))
-
+    pass_x(0, far(2))
+    pass_x(0, far(3))
     @pl.when(seg == 0)
     def _():
         fold_four(1, nears)
+
+    @pl.when(seg == 0)
+    def _():
         fold_four(0, fars)
 
-    for i in range(2):
-        pass_x(1, far(i))
-
+    pass_x(1, far(0))
+    pass_x(1, far(1))
+    pass_x(1, far(2))
     @pl.when(seg == 0)
     def _():
         pl.semaphore_wait(y_all, N_HEAD - 1)
         hand_over(0)
 
-    for i in range(2, FAR):
-        pass_x(1, far(i))
-
+    pass_x(1, far(3))
     @pl.when(seg == 0)
     def _():
         fold_four(1, fars)
@@ -565,7 +610,9 @@
         for m in range(MICRO):
             for z_at in range(NZ):
                 wait_s(m, z_at)
+            inverse_copy(m).wait()
         for m in range(MICRO):
+            cut_windows(m)
             for h in range(N_HEAD):
                 n_arrival(m, h).wait_recv()
             total = ss_in[m, 0]
@@ -573,21 +620,32 @@
                 total = total + ss_in[m, h]
             wide_total = jnp.broadcast_to(total[:, :ROWS], (HEAD_DIM, ROWS))
             norm = lax.rsqrt(jnp.transpose(wide_total) / FEATURES + 1e-05)
-            kx, vx = gathered(m, range(NZ))
+            for h in range(HEADS_LOCAL):
+                a_copy(m, h).wait_recv()
+                lifted = (
+                    q_ref[m, :, h * HEAD_DIM : (h + 1) * HEAD_DIM].astype(jnp.float32)
+                    + att[m, h].astype(jnp.float32) * norm
+                ).astype(jnp.bfloat16)
+                for own in range(2):
+                    rows = slice(own * GROUP_ROWS + h * BLOCK, own * GROUP_ROWS + (h + 1) * BLOCK)
+                    part = slice(own * BLOCK, (own + 1) * BLOCK)
+                    qx[m, rows, :HEAD_DIM] = lifted[part]
+                    qx[m, rows, HEAD_DIM:] = query_mask[m, part, :]
             scores = []
-            for rows in groups:
-                for h in range(rows.start // ROWS, rows.stop // ROWS):
-                    a_copy(m, h).wait_recv()
-                    lifted = (
-                        q_ref[m, :, h * HEAD_DIM : (h + 1) * HEAD_DIM].astype(jnp.float32)
-                        + att[m, h].astype(jnp.float32) * norm
-                    )
-                    stage_query(m, h, lifted.astype(jnp.bfloat16))
+            for own, rows in enumerate(groups):
+                kx = jnp.concatenate([k_win[m, own], b_win[m, own]], axis=1)
                 scores.append(score(m, rows, kx))
-            for rows, one in zip(groups, scores):
-                settle(m, vx, rows, one)
+            for own, rows in enumerate(groups):
+                values = v_win[m, own]
+                vx = jnp.concatenate([values, jnp.ones_like(values)], axis=1)
+                settle(m, vx, rows, scores[own])
             for h in range(HEADS_LOCAL):
-                put(m, h, finished(m, h))
+                for own in range(2):
+                    rows = slice(own * GROUP_ROWS + h * BLOCK, own * GROUP_ROWS + (h + 1) * BLOCK)
+                    out = acc[m, rows, :HEAD_DIM] / acc[m, rows, HEAD_DIM:]
+                    o_ref[
+                        0, m, own * BLOCK : (own + 1) * BLOCK, h * HEAD_DIM : (h + 1) * HEAD_DIM
+                    ] = out.astype(jnp.bfloat16)
 
     for m in range(MICRO):
         finish_sends(m)
@@ -610,8 +668,8 @@
             pltpu.SMEM((MICRO, 64), jnp.int32),
             pltpu.SMEM((MICRO, DOCS), jnp.int32),
             pltpu.VMEM((MICRO, ROWS, HEADS_LOCAL * HEAD_DIM), jnp.bfloat16),
-            pltpu.VMEM((MICRO, 2, NZ, 2, 2, ROWS, HEAD_DIM), jnp.bfloat16),
-            pltpu.VMEM((MICRO, NZ, 2, 2, ROWS, 128), jnp.bfloat16),
+            pltpu.VMEM((MICRO, 2, NZ, 2, 2, 2, BLOCK, HEAD_DIM), jnp.bfloat16),
+            pltpu.VMEM((MICRO, NZ, 2, 2, 2, BLOCK, 128), jnp.bfloat16),
             pltpu.VMEM((MICRO, ROWS, 128), jnp.bfloat16),
             pltpu.VMEM((MICRO, rows, 256), jnp.bfloat16),
             pltpu.VMEM((MICRO, rows, 256), jnp.float32),
@@ -619,8 +677,14 @@
             pltpu.VMEM((MICRO, HEADS_LOCAL, ROWS, HEAD_DIM), jnp.bfloat16),
             pltpu.VMEM((MICRO, 1, 128), jnp.float32),
             pltpu.VMEM((MICRO, N_HEAD, 1, 128), jnp.float32),
-            dma((MICRO, 3)),
+            pltpu.VMEM((MICRO, 1, 128), jnp.int32),
+            pltpu.SMEM((MICRO, 1, 128), jnp.int32),
+            pltpu.VMEM((MICRO, 2, WINDOW * BLOCK, HEAD_DIM), jnp.bfloat16),
+            pltpu.VMEM((MICRO, 2, WINDOW * BLOCK, HEAD_DIM), jnp.bfloat16),
+            pltpu.VMEM((MICRO, 2, WINDOW * BLOCK, 128), jnp.bfloat16),
+            dma((MICRO, 5)),
             dma((2,)),
+            dma((MICRO,)),
             dma((MICRO, NZ)),
             dma((MICRO, NZ)),
             dma((MICRO, 2, 2)),

time: 41 us -> 40.2 us (0.980)
  Pallas kernels: 40.2 us -> 39.2 us
    pallas_call x1, Pallas kernels: 40.2 us -> 39.2 us  [on_device(): pl.pallas_call(kernel, out_shape=jax.ShapeDtypeStruct(queries.shape, jnp....]
where the time goes in v6:
time: 40.2 us; the launch traced here: 39.9 us
  Pallas kernels  39.2 us (98%)
  local copies, waits for them, and re-layouts  0.71 us (2%)
    pallas_call x1, Pallas kernels, on_device(): pl.pallas_call(kernel, out_shape=jax.ShapeDtypeStruct(queries.shape, jnp....  39.2 us

profile of v6, /device:TPU:2, one launch (start us, length us, event | category | flops | bytes accessed | tf_op | source)
XLA Modules:
  0.0 39.9 jit_solution(3031975952462364559)
XLA Ops:
  0.0 39.2 %attend_two_layers.1 = bf16[1,2,64,1024]{3,2,1,0:T(8,128)(2,1)S(1)} custom-call(s32[2,64]{1,0:T(2,128)} %order_hbm.1, s32[2,16]{1,0:T(2,128)} %lengths_hbm.1, bf16[1,2,64,1024]{3,2,1,0:T(8,128)(2,1)} %q_hbm.1, bf16[1,2,64,128]{3,2,1,0:T(8,128)(2,1)} %k_hbm.1, bf16[1,2,64,128]{3,2,1,0:T(8,128)(2,1)} %v_hbm.1), custom_call_target="tpu_custom_call" | custom-call | tf_op jit(solution)/shard_map/attend_two_layers/pallas_call | solution.py:662
  39.2 0.7 %copy.7 = bf16[1,2,64,1024]{3,2,1,0:T(8,128)(2,1)} copy(bf16[1,2,64,1024]{3,2,1,0:T(8,128)(2,1)S(1)} %attend_two_layers.1) | data formatting | bytes 524288

commit v7 on v6

--- a/solution.py
+++ b/solution.py
@@ -356,7 +356,7 @@
         slice(start, start + GROUP_ROWS) for start in range(0, HEADS_LOCAL * ROWS, GROUP_ROWS)
     ]
 
-    def fold(m, z_list):
+    def fold(m, z_list, last=False):
         kx, vx = gathered(m, z_list)
         scores = [score(m, rows, kx) for rows in groups]
         for rows, one in zip(groups, scores):
@@ -365,18 +365,21 @@
             peak[m, rows, :] = new
             weights = jnp.exp2((one - new[:, :1]) * EXP_SCALE).astype(jnp.bfloat16)
             fade = jnp.exp2((old - new) * EXP_SCALE)
-            acc[m, rows, :] = acc[m, rows, :] * jnp.concatenate([fade, fade], axis=1) + jnp.dot(
+            mixed = acc[m, rows, :] * jnp.concatenate([fade, fade], axis=1) + jnp.dot(
                 weights, vx, preferred_element_type=jnp.float32
             )
-
-    def settle(m, vx, rows, scores):
+            if last:
+                out = (mixed[:, :HEAD_DIM] / mixed[:, HEAD_DIM:]).astype(jnp.bfloat16)
+                for part in range(GROUP_ROWS // ROWS):
+                    att[m, rows.start // ROWS + part] = out[part * ROWS : (part + 1) * ROWS]
+            else:
+                acc[m, rows, :] = mixed
+
+    def settle(vx, scores):
         top = jnp.max(scores, axis=1, keepdims=True)
         weights = jnp.exp2((scores - top) * EXP_SCALE).astype(jnp.bfloat16)
-        acc[m, rows, :] = jnp.dot(weights, vx, preferred_element_type=jnp.float32)
-
-    def finished(m, h):
-        rows = slice(h * ROWS, (h + 1) * ROWS)
-        return (acc[m, rows, :HEAD_DIM] / acc[m, rows, HEAD_DIM:]).astype(jnp.bfloat16)
+        mixed = jnp.dot(weights, vx, preferred_element_type=jnp.float32)
+        return (mixed[:, :HEAD_DIM] / mixed[:, HEAD_DIM:]).astype(jnp.bfloat16)
 
     def put(m, h, out):
         o_ref[0, m, :, h * HEAD_DIM : (h + 1) * HEAD_DIM] = out
@@ -419,9 +422,7 @@
     def hand_over(m):
         squares = jnp.zeros((ROWS, HEAD_DIM), jnp.float32)
         for h in range(HEADS_LOCAL):
-            out = finished(m, h)
-            att[m, h] = out
-            wide = out.astype(jnp.float32)
+            wide = att[m, h].astype(jnp.float32)
             squares = squares + wide * wide
         ss_out[m, :, :ROWS] = jnp.sum(jnp.transpose(squares), axis=0, keepdims=True)
         for h in range(N_HEAD):
@@ -460,10 +461,10 @@
 
             lax.fori_loop(0, WINDOW, one_block, 0, unroll=3)
 
-    def fold_four(m, z_list):
+    def fold_four(m, z_list, last=False):
         for z_at in z_list:
             wait_s(m, z_at)
-        fold(m, z_list)
+        fold(m, z_list, last)
 
     def prepare(m):
         build_masks(m)
@@ -482,14 +483,20 @@
     for m in range(MICRO):
         for one in loads[m][:4]:
             one.wait()
-        for i in range(FAR):
+        for i in (2, 3, 0, 1):
             @pl.when((far(i) < z) & direct(i))
             def _():
                 z_send_copy(m, far(i)).start()
+    for m in range(MICRO):
         for i in range(1, FAR):
             @pl.when(near(i) < z)
             def _():
                 z_send_copy(m, near(i)).start()
+    @pl.when(xh == 1)
+    def _():
+        for m in range(MICRO):
+            x_copy(m, z, xh).start()
+
     def answer_near(i):
         @pl.when(near(i) > z)
         def _():
@@ -507,12 +514,13 @@
     def _():
         pl.semaphore_wait(x_in, 1)
 
+        for m in range(MICRO):
+            x_copy(m, z, xh).start()
+
     @pl.when(core == 1)
     def _():
         pl.semaphore_wait(s_in, 1)
 
-    for m in range(MICRO):
-        x_copy(m, z, xh).start()
     answer_near(3)
     prepare(1)
     for i in range(1, FAR):
@@ -585,7 +593,7 @@
 
     @pl.when(seg == 0)
     def _():
-        fold_four(0, fars)
+        fold_four(0, fars, last=True)
 
     pass_x(1, far(0))
     pass_x(1, far(1))
@@ -598,7 +606,7 @@
     pass_x(1, far(3))
     @pl.when(seg == 0)
     def _():
-        fold_four(1, fars)
+        fold_four(1, fars, last=True)
         hand_over(1)
         for m in range(MICRO):
             for h in range(HEADS_LOCAL):
@@ -613,6 +621,11 @@
             inverse_copy(m).wait()
         for m in range(MICRO):
             cut_windows(m)
+            for own in range(2):
+                part = slice(own * BLOCK, (own + 1) * BLOCK)
+                for h in range(HEADS_LOCAL):
+                    rows = slice(own * GROUP_ROWS + h * BLOCK, own * GROUP_ROWS + (h + 1) * BLOCK)
+                    qx[m, rows, HEAD_DIM:] = query_mask[m, part, :]
             for h in range(N_HEAD):
                 n_arrival(m, h).wait_recv()
             total = ss_in[m, 0]
@@ -630,7 +643,6 @@
                     rows = slice(own * GROUP_ROWS + h * BLOCK, own * GROUP_ROWS + (h + 1) * BLOCK)
                     part = slice(own * BLOCK, (own + 1) * BLOCK)
                     qx[m, rows, :HEAD_DIM] = lifted[part]
-                    qx[m, rows, HEAD_DIM:] = query_mask[m, part, :]
             scores = []
             for own, rows in enumerate(groups):
                 kx = jnp.concatenate([k_win[m, own], b_win[m, own]], axis=1)
@@ -638,14 +650,11 @@
             for own, rows in enumerate(groups):
                 values = v_win[m, own]
                 vx = jnp.concatenate([values, jnp.ones_like(values)], axis=1)
-                settle(m, vx, rows, scores[own])
-            for h in range(HEADS_LOCAL):
-                for own in range(2):
-                    rows = slice(own * GROUP_ROWS + h * BLOCK, own * GROUP_ROWS + (h + 1) * BLOCK)
-                    out = acc[m, rows, :HEAD_DIM] / acc[m, rows, HEAD_DIM:]
+                out = settle(vx, scores[own])
+                for h in range(HEADS_LOCAL):
                     o_ref[
                         0, m, own * BLOCK : (own + 1) * BLOCK, h * HEAD_DIM : (h + 1) * HEAD_DIM
-                    ] = out.astype(jnp.bfloat16)
+                    ] = out[h * BLOCK : (h + 1) * BLOCK]
 
     for m in range(MICRO):
         finish_sends(m)

time: 40.2 us -> 39.9 us (level)
  no operation moved by 1% of the time
where the time goes in v7:
time: 39.9 us; the launch traced here: 39.8 us
  Pallas kernels  39.1 us (98%)
  local copies, waits for them, and re-layouts  0.71 us (2%)
    pallas_call x1, Pallas kernels, on_device(): pl.pallas_call(kernel, out_shape=jax.ShapeDtypeStruct(queries.shape, jnp....  39.1 us

profile of v7, /device:TPU:2, one launch (start us, length us, event | category | flops | bytes accessed | tf_op | source)
XLA Modules:
  0.0 39.8 jit_solution(14392681312441985305)
XLA Ops:
  0.0 39.1 %attend_two_layers.1 = bf16[1,2,64,1024]{3,2,1,0:T(8,128)(2,1)S(1)} custom-call(s32[2,64]{1,0:T(2,128)} %order_hbm.1, s32[2,16]{1,0:T(2,128)} %lengths_hbm.1, bf16[1,2,64,1024]{3,2,1,0:T(8,128)(2,1)} %q_hbm.1, bf16[1,2,64,128]{3,2,1,0:T(8,128)(2,1)} %k_hbm.1, bf16[1,2,64,128]{3,2,1,0:T(8,128)(2,1)} %v_hbm.1), custom_call_target="tpu_custom_call" | custom-call | tf_op jit(solution)/shard_map/attend_two_layers/pallas_call | solution.py:671
  39.1 0.7 %copy.7 = bf16[1,2,64,1024]{3,2,1,0:T(8,128)(2,1)} copy(bf16[1,2,64,1024]{3,2,1,0:T(8,128)(2,1)S(1)} %attend_two_layers.1) | data formatting | bytes 524288

commit v8 on v7

--- a/solution.py
+++ b/solution.py
@@ -333,10 +333,6 @@
 
         lax.fori_loop(0, NZ, one_z, 0)
 
-    def start_rows(m):
-        acc[m] = jnp.zeros((HEADS_LOCAL * ROWS, 256), jnp.float32)
-        peak[m] = jnp.full((HEADS_LOCAL * ROWS, 128), HIDDEN, jnp.float32)
-
     def gathered(m, z_list):
         keys, values = [], []
         for z_at in z_list:
@@ -357,23 +353,26 @@
     ]
 
     def fold(m, z_list, last=False):
+        opening = not last
         kx, vx = gathered(m, z_list)
         scores = [score(m, rows, kx) for rows in groups]
         for rows, one in zip(groups, scores):
+            if opening:
+                top = jnp.max(one, axis=1, keepdims=True)
+                weights = jnp.exp2((one - top) * EXP_SCALE).astype(jnp.bfloat16)
+                peak[m, rows, :] = jnp.broadcast_to(top, (GROUP_ROWS, 128))
+                acc[m, rows, :] = jnp.dot(weights, vx, preferred_element_type=jnp.float32)
+                continue
             old = peak[m, rows, :]
             new = jnp.maximum(old, jnp.max(one, axis=1, keepdims=True))
-            peak[m, rows, :] = new
             weights = jnp.exp2((one - new[:, :1]) * EXP_SCALE).astype(jnp.bfloat16)
             fade = jnp.exp2((old - new) * EXP_SCALE)
             mixed = acc[m, rows, :] * jnp.concatenate([fade, fade], axis=1) + jnp.dot(
                 weights, vx, preferred_element_type=jnp.float32
             )
-            if last:
-                out = (mixed[:, :HEAD_DIM] / mixed[:, HEAD_DIM:]).astype(jnp.bfloat16)
-                for part in range(GROUP_ROWS // ROWS):
-                    att[m, rows.start // ROWS + part] = out[part * ROWS : (part + 1) * ROWS]
-            else:
-                acc[m, rows, :] = mixed
+            out = (mixed[:, :HEAD_DIM] / mixed[:, HEAD_DIM:]).astype(jnp.bfloat16)
+            for part in range(GROUP_ROWS // ROWS):
+                att[m, rows.start // ROWS + part] = out[part * ROWS : (part + 1) * ROWS]
 
     def settle(vx, scores):
         top = jnp.max(scores, axis=1, keepdims=True)
@@ -476,7 +475,6 @@
 
         @pl.when(seg == 0)
         def _():
-            start_rows(m)
             for h in range(HEADS_LOCAL):
                 stage_query(m, h, q_ref[m, :, h * HEAD_DIM : (h + 1) * HEAD_DIM])
 

time: 39.9 us -> 39.9 us (level)
  the two profiles are of different devices: /device:TPU:2 before, /device:TPU:134 now
where the time goes in v8:
time: 39.9 us; the launch traced here: 39.8 us
  Pallas kernels  39.1 us (98%)
  local copies, waits for them, and re-layouts  0.71 us (2%)
    pallas_call x1, Pallas kernels, on_device(): pl.pallas_call(kernel, out_shape=jax.ShapeDtypeStruct(queries.shape, jnp....  39.1 us

profile of v8, /device:TPU:134, one launch (start us, length us, event | category | flops | bytes accessed | tf_op | source)
XLA Modules:
  0.0 39.8 jit_solution(549474229794317785)
XLA Ops:
  0.0 39.1 %attend_two_layers.1 = bf16[1,2,64,1024]{3,2,1,0:T(8,128)(2,1)S(1)} custom-call(s32[2,64]{1,0:T(2,128)} %order_hbm.1, s32[2,16]{1,0:T(2,128)} %lengths_hbm.1, bf16[1,2,64,1024]{3,2,1,0:T(8,128)(2,1)} %q_hbm.1, bf16[1,2,64,128]{3,2,1,0:T(8,128)(2,1)} %k_hbm.1, bf16[1,2,64,128]{3,2,1,0:T(8,128)(2,1)} %v_hbm.1), custom_call_target="tpu_custom_call" | custom-call | tf_op jit(solution)/shard_map/attend_two_layers/pallas_call | solution.py:669
  39.1 0.7 %copy.7 = bf16[1,2,64,1024]{3,2,1,0:T(8,128)(2,1)} copy(bf16[1,2,64,1024]{3,2,1,0:T(8,128)(2,1)S(1)} %attend_two_layers.1) | data formatting | bytes 524288

commit v9 on v8

--- a/solution.py
+++ b/solution.py
@@ -428,9 +428,6 @@
             n_copy(m, h).start()
         for h in range(HEADS_LOCAL):
             a_copy(m, h).start()
-        for h in range(HEADS_LOCAL):
-            put(m, h, att[m, h])
-
     def inverse_copy(m):
         return pltpu.make_async_copy(inverse_v.at[m], inverse.at[m], inverse_sem.at[m])
 
@@ -606,6 +603,9 @@
     def _():
         fold_four(1, fars, last=True)
         hand_over(1)
+        for m in range(MICRO):
+            for h in range(HEADS_LOCAL):
+                put(m, h, att[m, h])
         for m in range(MICRO):
             for h in range(HEADS_LOCAL):
                 a_copy(m, h).wait_send()

time: 39.9 us -> 39.9 us (level)
  no operation moved by 1% of the time
where the time goes in v9:
time: 39.9 us; the launch traced here: 39.8 us
  Pallas kernels  39.1 us (98%)
  local copies, waits for them, and re-layouts  0.71 us (2%)
    pallas_call x1, Pallas kernels, on_device(): pl.pallas_call(kernel, out_shape=jax.ShapeDtypeStruct(queries.shape, jnp....  39.1 us

profile of v9, /device:TPU:134, one launch (start us, length us, event | category | flops | bytes accessed | tf_op | source)
XLA Modules:
  0.0 39.8 jit_solution(13697279416259265376)
XLA Ops:
  0.0 39.1 %attend_two_layers.1 = bf16[1,2,64,1024]{3,2,1,0:T(8,128)(2,1)S(1)} custom-call(s32[2,64]{1,0:T(2,128)} %order_hbm.1, s32[2,16]{1,0:T(2,128)} %lengths_hbm.1, bf16[1,2,64,1024]{3,2,1,0:T(8,128)(2,1)} %q_hbm.1, bf16[1,2,64,128]{3,2,1,0:T(8,128)(2,1)} %k_hbm.1, bf16[1,2,64,128]{3,2,1,0:T(8,128)(2,1)} %v_hbm.1), custom_call_target="tpu_custom_call" | custom-call | tf_op jit(solution)/shard_map/attend_two_layers/pallas_call | solution.py:669
  39.1 0.7 %copy.7 = bf16[1,2,64,1024]{3,2,1,0:T(8,128)(2,1)} copy(bf16[1,2,64,1024]{3,2,1,0:T(8,128)(2,1)S(1)} %attend_two_layers.1) | data formatting | bytes 524288

commit v10 on v7

--- a/solution.py
+++ b/solution.py
@@ -425,7 +425,7 @@
             wide = att[m, h].astype(jnp.float32)
             squares = squares + wide * wide
         ss_out[m, :, :ROWS] = jnp.sum(jnp.transpose(squares), axis=0, keepdims=True)
-        for h in range(N_HEAD):
+        for h in (0, 1, 7, 2, 6, 3, 5, 4):
             n_copy(m, h).start()
         for h in range(HEADS_LOCAL):
             a_copy(m, h).start()

time: 39.9 us -> 39.9 us (level)
  no operation moved by 1% of the time
where the time goes in v10:
time: 39.9 us; the launch traced here: 39.8 us
  Pallas kernels  39.1 us (98%)
  local copies, waits for them, and re-layouts  0.71 us (2%)
    pallas_call x1, Pallas kernels, on_device(): pl.pallas_call(kernel, out_shape=jax.ShapeDtypeStruct(queries.shape, jnp....  39.1 us

profile of v10, /device:TPU:2, one launch (start us, length us, event | category | flops | bytes accessed | tf_op | source)
XLA Modules:
  0.0 39.8 jit_solution(16066457370280689089)
XLA Ops:
  0.0 39.1 %attend_two_layers.1 = bf16[1,2,64,1024]{3,2,1,0:T(8,128)(2,1)S(1)} custom-call(s32[2,64]{1,0:T(2,128)} %order_hbm.1, s32[2,16]{1,0:T(2,128)} %lengths_hbm.1, bf16[1,2,64,1024]{3,2,1,0:T(8,128)(2,1)} %q_hbm.1, bf16[1,2,64,128]{3,2,1,0:T(8,128)(2,1)} %k_hbm.1, bf16[1,2,64,128]{3,2,1,0:T(8,128)(2,1)} %v_hbm.1), custom_call_target="tpu_custom_call" | custom-call | tf_op jit(solution)/shard_map/attend_two_layers/pallas_call | solution.py:671
  39.1 0.7 %copy.7 = bf16[1,2,64,1024]{3,2,1,0:T(8,128)(2,1)} copy(bf16[1,2,64,1024]{3,2,1,0:T(8,128)(2,1)S(1)} %attend_two_layers.1) | data formatting | bytes 524288
